TPU v7x, 32 devices: a whole 2x2x4 slice. The times are simulated.
32 devices in a mesh: dp: 8 (over y, x, core), proto: 4 (over z).
Axes of the slice: x: 2, y: 2, z: 4, core: 2. Of those that a mesh axis runs over, the one named last changes fastest.
Arguments:
- student_feats: float32 [1280, 256], P('dp'), may hold values from -6 to 6
- teacher_feats: float32 [256, 256], P('dp'), may hold values from -6 to 6
- student_proto: float32 [256, 32768], P('dp', 'proto'), may hold values from -6 to 6
- teacher_proto: float32 [256, 32768], P('dp', 'proto'), may hold values from -6 to 6
- crops: int32 [1280, 2], P('dp'), may hold values from 0 to 15, as said below
- step: int32 [1], replicated, may hold values from 0 to 24999
Outputs:
- student_next: float32 [256, 32768], P('dp', 'proto')
- teacher_next: float32 [256, 32768], P('dp', 'proto')
- feature_grad: float32 [1280, 256], P('dp')
Inputs may be any that keep to these rules, and one draw needn't show every extreme that they name: Within each device's block of 160 rows every pair (image i < 16, slot c < 10) appears exactly once; slots below 2 are the global crops, slot g of image i being the same crop as teacher row 2 * i + g of that block.
All inputs are finite; a program needn't handle non-finite values.
Results may differ from a plain program's by a relative error of at most 0.0003.
Values sent between devices are 32-bit elements; how exact they have to be, the bound alone decides.
A program may use at most 128 MiB of HBM per device.

v0:
```python
import jax
import jax.numpy as jnp
from jax import lax
from jax.sharding import PartitionSpec as P

CROPS = 10
GLOBAL_CROPS = 2
ITERS = 3
WARM_STEPS = 12500
TOTAL_STEPS = 625000


student_temp = 0.1
loss_scale = 16777216.0
norm_eps = 1e-06
square_eps = 1e-06
rate_peak = 0.05
weight_decay = 0.04
momentum_base = 0.994
highest = lax.Precision.HIGHEST


def plan(step):
    value = step[0].astype(jnp.float32)
    ramp = jnp.minimum(1.0, value / WARM_STEPS)
    rate = rate_peak * (0.25 + 0.75 * ramp)
    teacher_temp = 0.04 + 0.03 * ramp
    momentum = 1.0 - (1.0 - momentum_base) * (jnp.cos(jnp.pi * value / TOTAL_STEPS) + 1.0) * 0.5
    return (rate, teacher_temp, momentum)


def unit_rows(values):
    norm = jnp.sqrt(jnp.sum(values * values, axis=1, keepdims=True) + norm_eps)
    return (values / norm, norm)


def unit_columns(values):
    norm = jnp.sqrt(jnp.sum(values * values, axis=0, keepdims=True) + norm_eps)
    return (values / norm, norm)


def body(student_feats, teacher_feats, student_proto, teacher_proto, crops, step):
    rate, teacher_temp, momentum = plan(step)
    full_student, full_teacher = (
        lax.all_gather(student_proto, "dp", axis=0, tiled=True),
        lax.all_gather(teacher_proto, "dp", axis=0, tiled=True),
    )
    student_unit, student_norm = unit_columns(full_student)
    teacher_unit, teacher_norm = unit_columns(full_teacher)
    t_unit, t_norm = unit_rows(teacher_feats)
    s_unit, s_norm = unit_rows(student_feats)
    crop_rows, width = s_unit.shape
    teach_rows = t_unit.shape[0]
    blocks = crop_rows // teach_rows
    row_blocks = s_unit.reshape(blocks, teach_rows, width)

    def block_expo(rows):
        logits = (
            jnp.dot(rows, student_unit, precision=highest, preferred_element_type=jnp.float32)
            / student_temp
        )
        return jnp.exp(logits)

    expo_blocks = lax.map(block_expo, row_blocks)
    student_total = jnp.sum(expo_blocks, axis=2).reshape(crop_rows)
    student_total = lax.psum(student_total, "proto")
    assign = jnp.exp(
        jnp.dot(t_unit, teacher_unit, precision=highest, preferred_element_type=jnp.float32)
        / teacher_temp
    )
    for turn in range(ITERS):
        column = lax.psum(jnp.sum(assign, axis=0), "dp")
        assign = assign / column[None, :]
        row_part = jnp.sum(assign, axis=1)
        if turn == 0:
            row = lax.psum(row_part, "proto")
        else:
            row = lax.psum(row_part, "proto")
        assign = assign / row[:, None]
    images = teach_rows // GLOBAL_CROPS * lax.axis_size("dp")
    pair_total = GLOBAL_CROPS * (GLOBAL_CROPS - 1) + (CROPS - GLOBAL_CROPS) * GLOBAL_CROPS
    coef = loss_scale / (pair_total * images * student_temp)
    teach_iota = lax.broadcasted_iota(jnp.int32, (1, teach_rows), 1)
    same = crops[:, 0:1] == teach_iota // GLOBAL_CROPS
    other = crops[:, 1:2] != teach_iota % GLOBAL_CROPS
    pairs = jnp.where(same & other, 1.0, 0.0).astype(jnp.float32)
    pair_blocks = pairs.reshape(blocks, teach_rows, teach_rows)
    total_blocks = student_total.reshape(blocks, teach_rows, 1)

    def grad_block(carry, pieces):
        rows, expo, pair_rows, total = pieces
        prob = expo / total
        target = jnp.dot(pair_rows, assign, precision=highest, preferred_element_type=jnp.float32)
        count = jnp.sum(pair_rows, axis=1, keepdims=True)
        dscore = coef * (count * prob - target)
        carry = carry + jnp.dot(
            rows.T, dscore, precision=highest, preferred_element_type=jnp.float32
        )
        back = jnp.dot(
            dscore, student_unit.T, precision=highest, preferred_element_type=jnp.float32
        )
        return (carry, back)

    start_grad = jnp.zeros(student_unit.shape, jnp.float32)
    grad_unit, backs = lax.scan(
        grad_block, start_grad, (row_blocks, expo_blocks, pair_blocks, total_blocks)
    )
    feature_part = backs.reshape(crop_rows, width)
    feature_unit = lax.psum(feature_part, "proto")
    feature_grad = (
        feature_unit - s_unit * jnp.sum(s_unit * feature_unit, axis=1, keepdims=True)
    ) / s_norm
    own_rows = student_proto.shape[0]
    first = lax.axis_index("dp") * own_rows
    own_unit = lax.dynamic_slice_in_dim(student_unit, first, own_rows, 0)
    part_grad = lax.psum_scatter(grad_unit, "dp", scatter_dimension=0, tiled=True)
    along_part = jnp.sum(own_unit * part_grad, axis=0)
    squares_part = jnp.sum(part_grad * part_grad, axis=0)
    along, squares = lax.psum((along_part, squares_part), "dp")
    proto_grad = (part_grad - own_unit * along[None, :]) / student_norm
    square = (squares - along * along)[None, :] / (student_norm * student_norm * width)
    direction = proto_grad / jnp.sqrt(square + square_eps)
    student_next = student_proto - rate * (direction + weight_decay * student_proto)
    teacher_next = momentum * teacher_proto + (1.0 - momentum) * student_next
    return (student_next, teacher_next, feature_grad)


def solution(mesh):
    in_specs = (
        P("dp", None),
        P("dp", None),
        P("dp", "proto"),
        P("dp", "proto"),
        P("dp", None),
        P(),
    )
    out_specs = (P("dp", "proto"), P("dp", "proto"), P("dp", None))
    return jax.shard_map(body, mesh=mesh, in_specs=in_specs, out_specs=out_specs, check_vma=False)
```

profile of v0, /device:TPU:0, one launch (start us, length us, event | category | flops | bytes accessed | tf_op | source)
XLA Modules:
  0.0 519.6 jit_solution(13586185951953333884)
XLA Ops:
  9.4 0.8 slice_reduce_fusion.1
  10.3 0.9 multiply_reduce_fusion.6
  11.2 1.0 multiply_reduce_fusion.5
  12.4 1.0 broadcast_divide_fusion.1
  13.4 53.6 %all-gather.5.cloned.1.call-done = f32[256,8192]{1,0:T(8,128)} async-done(((f32[32,8192]{1,0:T(8,128)}), f32[256,8192]{1,0:T(8,128)}) %all-gather.5.cloned.1.call-update) | async-done | bytes 8388624 | tf_op jit(solution)/shard_map/all_gather | solution.py:46
  67.0 4.2 multiply_reduce_fusion
  71.3 1.5 copy-done.2
  72.8 5.2 %fusion.32 = (f32[8192]{0:T(1024)S(1)}, f32[32,8192]{1,0:T(8,128)S(1)}) fusion(f32[]{:T(128)} %bitcast.4, f32[256,8192]{1,0:T(8,128)S(1)} %copy-done.2, f32[8192]{0:T(1024)S(1)} %add_sqrt_fusion, f32[32,256]{1,0:T(8,128)S(1)} %copy-done.6, f32[32]{0:T(128)S(1)} %add_sqrt_fusion.3), kind=kOutput, calls=%fused_computation.68 | convolution fusion | flops 807927808 | bytes 9535620 | tf_op jit(solution)/shard_map/dot_general | solution.py:68
  78.0 24.1 %psum.71 = f32[8192]{0:T(1024)S(1)} all-reduce(f32[8192]{0:T(1024)S(1)} %get-tuple-element.142), channel_id=1, replica_groups=mesh['dp'=8,'proto'=4] {'dp'}, use_global_device_ids=true, to_apply=%region_9.10 | all-reduce | flops 8192 | bytes 65536 | tf_op jit(solution)/shard_map/psum | solution.py:72
  102.3 11.7 %psum.72 = f32[32]{0:T(128)S(1)} all-reduce(f32[32]{0:T(128)S(1)} %divide_reduce_fusion), channel_id=1, replica_groups=mesh['dp'=8,'proto'=4] {'proto'}, use_global_device_ids=true, to_apply=%region_11.12 | all-reduce | flops 32 | bytes 256 | tf_op jit(solution)/shard_map/psum | solution.py:76
  114.3 22.6 %psum.73 = f32[8192]{0:T(1024)S(1)} all-reduce(f32[8192]{0:T(1024)S(1)} %fusion.26), channel_id=1, replica_groups=mesh['dp'=8,'proto'=4] {'dp'}, use_global_device_ids=true, to_apply=%region_13.14 | all-reduce | flops 8192 | bytes 65536 | tf_op jit(solution)/shard_map/psum | solution.py:72
  137.2 8.4 %psum.74 = f32[32]{0:T(128)S(1)} all-reduce(f32[32]{0:T(128)S(1)} %fusion.27), channel_id=1, replica_groups=mesh['dp'=8,'proto'=4] {'proto'}, use_global_device_ids=true, to_apply=%region_15.16 | all-reduce | flops 32 | bytes 256 | tf_op jit(solution)/shard_map/psum | solution.py:78
  145.9 22.5 %psum.75 = f32[8192]{0:T(1024)S(1)} all-reduce(f32[8192]{0:T(1024)S(1)} %fusion.28), channel_id=1, replica_groups=mesh['dp'=8,'proto'=4] {'dp'}, use_global_device_ids=true, to_apply=%region_17.18 | all-reduce | flops 8192 | bytes 65536 | tf_op jit(solution)/shard_map/psum | solution.py:72
  168.9 4.2 multiply_reduce_fusion.1
  173.2 1.5 copy-done.1
  174.7 4.2 broadcast_divide_fusion
  178.8 46.2 %while.23 = (s32[]{:T(128)}, f32[5,32,8192]{2,1,0:T(8,128)}, f32[5,32,256]{2,1,0:T(8,128)S(1)}, f32[256,8192]{1,0:T(8,128)}, s32[]{:T(128)}) while((s32[]{:T(128)}, f32[5,32,8192]{2,1,0:T(8,128)}, f32[5,32,256]{2,1,0:T(8,128)S(1)}, f32[256,8192]{1,0:T(8,128)}, s32[]{:T(128)}) %tuple.62), condition=%wide.region_3.0_spmd, body=%wide.region_2.0_spmd.sunk | while | flops 805568512 | bytes 9471037 | solution.py:64
  178.8 9.3 %fusion.52 = f32[5,32,8192]{2,1,0:T(8,128)} fusion(f32[5,32,8192]{2,1,0:T(8,128)} %get-tuple-element.232, s32[]{:T(128)} %get-tuple-element.231, f32[256,8192]{1,0:T(8,128)} %get-tuple-element.239, f32[5,32,256]{2,1,0:T(8,128)S(1)} %get-tuple-element.238), kind=kOutput, calls=%fused_computation.3.clone.1 | convolution fusion | flops 805568512 | bytes 9470976 | tf_op jit(solution)/shard_map/while/body/eval_jaxpr/dot_general | solution.py:59
  188.1 9.2 %fusion.52 = f32[5,32,8192]{2,1,0:T(8,128)} fusion(f32[5,32,8192]{2,1,0:T(8,128)} %get-tuple-element.232, s32[]{:T(128)} %get-tuple-element.231, f32[256,8192]{1,0:T(8,128)} %get-tuple-element.239, f32[5,32,256]{2,1,0:T(8,128)S(1)} %get-tuple-element.238), kind=kOutput, calls=%fused_computation.3.clone.1 | convolution fusion | flops 805568512 | bytes 9470976 | tf_op jit(solution)/shard_map/while/body/eval_jaxpr/dot_general | solution.py:59
  197.3 9.2 %fusion.52 = f32[5,32,8192]{2,1,0:T(8,128)} fusion(f32[5,32,8192]{2,1,0:T(8,128)} %get-tuple-element.232, s32[]{:T(128)} %get-tuple-element.231, f32[256,8192]{1,0:T(8,128)} %get-tuple-element.239, f32[5,32,256]{2,1,0:T(8,128)S(1)} %get-tuple-element.238), kind=kOutput, calls=%fused_computation.3.clone.1 | convolution fusion | flops 805568512 | bytes 9470976 | tf_op jit(solution)/shard_map/while/body/eval_jaxpr/dot_general | solution.py:59
  206.5 9.2 %fusion.52 = f32[5,32,8192]{2,1,0:T(8,128)} fusion(f32[5,32,8192]{2,1,0:T(8,128)} %get-tuple-element.232, s32[]{:T(128)} %get-tuple-element.231, f32[256,8192]{1,0:T(8,128)} %get-tuple-element.239, f32[5,32,256]{2,1,0:T(8,128)S(1)} %get-tuple-element.238), kind=kOutput, calls=%fused_computation.3.clone.1 | convolution fusion | flops 805568512 | bytes 9470976 | tf_op jit(solution)/shard_map/while/body/eval_jaxpr/dot_general | solution.py:59
  215.8 9.3 %fusion.52 = f32[5,32,8192]{2,1,0:T(8,128)} fusion(f32[5,32,8192]{2,1,0:T(8,128)} %get-tuple-element.232, s32[]{:T(128)} %get-tuple-element.231, f32[256,8192]{1,0:T(8,128)} %get-tuple-element.239, f32[5,32,256]{2,1,0:T(8,128)S(1)} %get-tuple-element.238), kind=kOutput, calls=%fused_computation.3.clone.1 | convolution fusion | flops 805568512 | bytes 9470976 | tf_op jit(solution)/shard_map/while/body/eval_jaxpr/dot_general | solution.py:59
  225.0 2.8 reduce_sum.137
  227.9 10.6 %all-reduce.1 = (f32[5,32,1]{1,2,0:T(1,128)S(1)}, f32[32]{0:T(128)S(1)}) all-reduce(f32[5,32,1]{1,2,0:T(1,128)S(1)} %reshape.147, f32[32]{0:T(128)S(1)} %fusion.29), channel_id=1, replica_groups=mesh['dp'=8,'proto'=4] {'proto'}, use_global_device_ids=true, to_apply=%region_5.6 | all-reduce | flops 192 | bytes 1536 | tf_op jit(solution)/shard_map/psum | solution.py:66
  238.8 107.3 %while.24 = (s32[]{:T(128)}, f32[256,8192]{1,0:T(8,128)}, f32[5,32,256]{2,1,0:T(8,128)}, f32[5,32,256]{2,1,0:T(8,128)S(1)}, f32[5,32,32]{2,1,0:T(8,128)S(1)}, /*...) while((s32[]{:T(128)}, f32[256,8192]{1,0:T(8,128)}, ...), condition=%wide.region_22.23_spmd.clone, body=%wide.region_20.22_spmd.clone.sunk | while | flops 1716519936 | bytes 64052252 | solution.py:105
  238.9 2.3 fusion.60
  241.3 9.2 %convolution_add_fusion.2 = f32[256,8192]{1,0:T(8,128)} fusion(f32[32,8192]{1,0:T(8,128)S(1)} %fusion.60, f32[256,8192]{1,0:T(8,128)} %get-tuple-element.253, pred[]{:T(512)S(6)} %compare.10, f32[5,32,256]{2,1,0:T(8,128)S(1)} %get-tuple-element.266, s32[]{:T(128)} %get-tuple-element.252), kind=kOutput, calls=%fused_computation.7.clone.1 | convolution fusion | flops 809500672 | bytes 17858564 | tf_op jit(solution)/shard_map/while/body/eval_jaxpr/dot_general | solution.py:96
  250.5 8.0 %fusion.61 = f32[5,32,256]{2,1,0:T(8,128)} fusion(f32[5,32,256]{2,1,0:T(8,128)} %get-tuple-element.254, s32[]{:T(128)} %get-tuple-element.252, f32[32,8192]{1,0:T(8,128)S(1)} %fusion.60, f32[256,8192]{1,0:T(8,128)S(1)} %copy-done), kind=kOutput, calls=%fused_computation.11.clone.1 | convolution fusion | flops 805306368 | bytes 9470464 | tf_op jit(solution)/shard_map/while/body/eval_jaxpr/dot_general | solution.py:99
  258.5 2.3 fusion.60
  260.9 11.5 %convolution_add_fusion.2 = f32[256,8192]{1,0:T(8,128)} fusion(f32[32,8192]{1,0:T(8,128)S(1)} %fusion.60, f32[256,8192]{1,0:T(8,128)} %get-tuple-element.253, pred[]{:T(512)S(6)} %compare.10, f32[5,32,256]{2,1,0:T(8,128)S(1)} %get-tuple-element.266, s32[]{:T(128)} %get-tuple-element.252), kind=kOutput, calls=%fused_computation.7.clone.1 | convolution fusion | flops 809500672 | bytes 17858564 | tf_op jit(solution)/shard_map/while/body/eval_jaxpr/dot_general | solution.py:96
  272.4 8.0 %fusion.61 = f32[5,32,256]{2,1,0:T(8,128)} fusion(f32[5,32,256]{2,1,0:T(8,128)} %get-tuple-element.254, s32[]{:T(128)} %get-tuple-element.252, f32[32,8192]{1,0:T(8,128)S(1)} %fusion.60, f32[256,8192]{1,0:T(8,128)S(1)} %copy-done), kind=kOutput, calls=%fused_computation.11.clone.1 | convolution fusion | flops 805306368 | bytes 9470464 | tf_op jit(solution)/shard_map/while/body/eval_jaxpr/dot_general | solution.py:99
  280.5 2.3 fusion.60
  282.8 11.5 %convolution_add_fusion.2 = f32[256,8192]{1,0:T(8,128)} fusion(f32[32,8192]{1,0:T(8,128)S(1)} %fusion.60, f32[256,8192]{1,0:T(8,128)} %get-tuple-element.253, pred[]{:T(512)S(6)} %compare.10, f32[5,32,256]{2,1,0:T(8,128)S(1)} %get-tuple-element.266, s32[]{:T(128)} %get-tuple-element.252), kind=kOutput, calls=%fused_computation.7.clone.1 | convolution fusion | flops 809500672 | bytes 17858564 | tf_op jit(solution)/shard_map/while/body/eval_jaxpr/dot_general | solution.py:96
  294.3 8.0 %fusion.61 = f32[5,32,256]{2,1,0:T(8,128)} fusion(f32[5,32,256]{2,1,0:T(8,128)} %get-tuple-element.254, s32[]{:T(128)} %get-tuple-element.252, f32[32,8192]{1,0:T(8,128)S(1)} %fusion.60, f32[256,8192]{1,0:T(8,128)S(1)} %copy-done), kind=kOutput, calls=%fused_computation.11.clone.1 | convolution fusion | flops 805306368 | bytes 9470464 | tf_op jit(solution)/shard_map/while/body/eval_jaxpr/dot_general | solution.py:99
  302.4 2.3 fusion.60
  304.7 11.5 %convolution_add_fusion.2 = f32[256,8192]{1,0:T(8,128)} fusion(f32[32,8192]{1,0:T(8,128)S(1)} %fusion.60, f32[256,8192]{1,0:T(8,128)} %get-tuple-element.253, pred[]{:T(512)S(6)} %compare.10, f32[5,32,256]{2,1,0:T(8,128)S(1)} %get-tuple-element.266, s32[]{:T(128)} %get-tuple-element.252), kind=kOutput, calls=%fused_computation.7.clone.1 | convolution fusion | flops 809500672 | bytes 17858564 | tf_op jit(solution)/shard_map/while/body/eval_jaxpr/dot_general | solution.py:96
  316.2 8.0 %fusion.61 = f32[5,32,256]{2,1,0:T(8,128)} fusion(f32[5,32,256]{2,1,0:T(8,128)} %get-tuple-element.254, s32[]{:T(128)} %get-tuple-element.252, f32[32,8192]{1,0:T(8,128)S(1)} %fusion.60, f32[256,8192]{1,0:T(8,128)S(1)} %copy-done), kind=kOutput, calls=%fused_computation.11.clone.1 | convolution fusion | flops 805306368 | bytes 9470464 | tf_op jit(solution)/shard_map/while/body/eval_jaxpr/dot_general | solution.py:99
  324.3 2.3 fusion.60
  326.6 11.5 %convolution_add_fusion.2 = f32[256,8192]{1,0:T(8,128)} fusion(f32[32,8192]{1,0:T(8,128)S(1)} %fusion.60, f32[256,8192]{1,0:T(8,128)} %get-tuple-element.253, pred[]{:T(512)S(6)} %compare.10, f32[5,32,256]{2,1,0:T(8,128)S(1)} %get-tuple-element.266, s32[]{:T(128)} %get-tuple-element.252), kind=kOutput, calls=%fused_computation.7.clone.1 | convolution fusion | flops 809500672 | bytes 17858564 | tf_op jit(solution)/shard_map/while/body/eval_jaxpr/dot_general | solution.py:96
  338.1 8.0 %fusion.61 = f32[5,32,256]{2,1,0:T(8,128)} fusion(f32[5,32,256]{2,1,0:T(8,128)} %get-tuple-element.254, s32[]{:T(128)} %get-tuple-element.252, f32[32,8192]{1,0:T(8,128)S(1)} %fusion.60, f32[256,8192]{1,0:T(8,128)S(1)} %copy-done), kind=kOutput, calls=%fused_computation.11.clone.1 | convolution fusion | flops 805306368 | bytes 9470464 | tf_op jit(solution)/shard_map/while/body/eval_jaxpr/dot_general | solution.py:99
  346.9 31.2 %all-reduce.5.cloned.1.call-done = f32[160,256]{1,0:T(8,128)} async-done(((f32[160,256]{1,0:T(8,128)}), f32[160,256]{1,0:T(8,128)}) %all-reduce.5.cloned.1.call-update) | async-done | bytes 163856 | tf_op jit(solution)/shard_map/psum | solution.py:109
  378.1 1.1 multiply_reduce_fusion.4
  379.2 73.6 %reduce-scatter.2.cloned.1.call-done = f32[32,8192]{1,0:T(8,128)} async-done(((f32[256,8192]{1,0:T(8,128)}), f32[32,8192]{1,0:T(8,128)}) %reduce-scatter.2.cloned.1.call-update) | async-done | bytes 1048592 | tf_op jit(solution)/shard_map/reduce_scatter | solution.py:116
  452.8 2.4 multiply_reduce_fusion.3
  455.3 1.7 subtract_divide_fusion
  457.0 52.0 %all-reduce.7.cloned.1.call-done = (f32[8192]{0:T(1024)}, f32[8192]{0:T(1024)}) async-done(((f32[8192]{0:T(1024)}, f32[8192]{0:T(1024)}), (f32[8192]{0:T(1024)}, f32[8192]{0:T(1024)})) %all-reduce.7.cloned.1.call-update) | async-done | bytes 65552 | tf_op jit(solution)/shard_map/psum | solution.py:119
  509.0 0.8 sqrt_multiply_fusion
  509.8 3.2 multiply_add_fusion
  (59 shorter events, 5.0 us)
Async XLA Ops:
  7.2 64.1 %copy-start.6 = (f32[32,256]{1,0:T(8,128)S(1)}, f32[32,256]{1,0:T(8,128)}, u32[]{:S(2)}) copy-start(f32[32,256]{1,0:T(8,128)} %param.11) | copy-start | bytes 98308
  7.2 59.8 %all-gather.5.cloned.1.call-start = ((), (), s32[]{:S(2)}) async-start(), calls=%async_computation.2 | async-start | bytes 9437184 | tf_op jit(solution)/shard_map/all_gather | solution.py:46
  7.9 161.0 %all-gather.3.cloned.1.call-start = ((), (), s32[]{:S(2)}) async-start(), calls=%async_computation.1 | async-start | bytes 9437184 | tf_op jit(solution)/shard_map/all_gather | solution.py:45
  8.7 369.4 %all-reduce.5.cloned.1.call-start = ((), (), s32[]{:S(2)}) async-start(), calls=%async_computation.4 | async-start | bytes 327680 | tf_op jit(solution)/shard_map/psum | solution.py:109
  67.0 5.8 %copy-start.2 = (f32[256,8192]{1,0:T(8,128)S(1)}, f32[256,8192]{1,0:T(8,128)}, u32[]{:S(2)}) copy-start(f32[256,8192]{1,0:T(8,128)} %all-gather.5.cloned.1.call-done) | copy-start | bytes 25165828
  168.9 5.8 %copy-start.1 = (f32[256,8192]{1,0:T(8,128)S(1)}, f32[256,8192]{1,0:T(8,128)}, u32[]{:S(2)}) copy-start(f32[256,8192]{1,0:T(8,128)} %all-gather.3.cloned.1.call-done) | copy-start | bytes 25165828
  241.3 9.2 %copy-start = (f32[256,8192]{1,0:T(8,128)S(1)}, f32[256,8192]{1,0:T(8,128)}, u32[]{:S(2)}) copy-start(f32[256,8192]{1,0:T(8,128)} %get-tuple-element.271) | copy-start | bytes 25165828 | tf_op jit(solution)/shard_map/while
  260.9 11.5 %copy-start = (f32[256,8192]{1,0:T(8,128)S(1)}, f32[256,8192]{1,0:T(8,128)}, u32[]{:S(2)}) copy-start(f32[256,8192]{1,0:T(8,128)} %get-tuple-element.271) | copy-start | bytes 25165828 | tf_op jit(solution)/shard_map/while
  282.8 11.5 %copy-start = (f32[256,8192]{1,0:T(8,128)S(1)}, f32[256,8192]{1,0:T(8,128)}, u32[]{:S(2)}) copy-start(f32[256,8192]{1,0:T(8,128)} %get-tuple-element.271) | copy-start | bytes 25165828 | tf_op jit(solution)/shard_map/while
  304.7 11.5 %copy-start = (f32[256,8192]{1,0:T(8,128)S(1)}, f32[256,8192]{1,0:T(8,128)}, u32[]{:S(2)}) copy-start(f32[256,8192]{1,0:T(8,128)} %get-tuple-element.271) | copy-start | bytes 25165828 | tf_op jit(solution)/shard_map/while
  326.6 11.5 %copy-start = (f32[256,8192]{1,0:T(8,128)S(1)}, f32[256,8192]{1,0:T(8,128)}, u32[]{:S(2)}) copy-start(f32[256,8192]{1,0:T(8,128)} %get-tuple-element.271) | copy-start | bytes 25165828 | tf_op jit(solution)/shard_map/while
  346.1 32.0 %copy-start.5 = (f32[160,256]{1,0:T(8,128)S(1)}, f32[160,256]{1,0:T(8,128)}, u32[]{:S(2)}) copy-start(f32[160,256]{1,0:T(8,128)} %param.10) | copy-start | bytes 491524
  346.1 163.7 %copy-start.3 = (f32[32,8192]{1,0:T(8,128)S(1)}, f32[32,8192]{1,0:T(8,128)}, u32[]{:S(2)}) copy-start(f32[32,8192]{1,0:T(8,128)} %param.13) | copy-start | bytes 3145732
  346.1 163.7 %copy-start.4 = (f32[32,8192]{1,0:T(8,128)S(1)}, f32[32,8192]{1,0:T(8,128)}, u32[]{:S(2)}) copy-start(f32[32,8192]{1,0:T(8,128)} %param.12) | copy-start | bytes 3145732
  346.1 106.7 %reduce-scatter.2.cloned.1.call-start = ((), (), s32[]{:S(2)}) async-start(), calls=%async_computation.3 | async-start | bytes 9437184 | tf_op jit(solution)/shard_map/reduce_scatter | solution.py:116
  346.7 162.3 %all-reduce.7.cloned.1.call-start = ((), (), s32[]{:S(2)}) async-start(), calls=%async_computation.5 | async-start | bytes 131072 | tf_op jit(solution)/shard_map/psum | solution.py:119
Sparse Core Ops, SparseCore 0:
  9.9 57.0 all-gather.4
  68.9 54.6 all-gather.2
  346.2 31.7 all-reduce.4
  381.8 70.9 reduce-scatter.1
  456.3 52.6 all-reduce.6
where the time goes:
time: 521 us; the launch traced here: 520 us
  waiting for transfers between devices  212 us (41%)
  matrix products  158 us (30%)
  blocking collectives  99.8 us (19%)
  other arithmetic  30.3 us (6%)
  between operations  14.7 us (3%)
    reduce_scatter x1, waiting for transfers between devices, body(): lax.psum_scatter(grad_unit, 'dp', scatter_dimension=0, tiled=True)  73.6 us
    psum x3, blocking collectives, body(): column = lax.psum(jnp.sum(assign, axis=0), 'dp')  69.2 us
    dot_general x5, matrix products, grad_block(): jnp.dot(rows.T, dscore, precision=highest, preferred_element_type=jnp.flo...  55.2 us
    all_gather x1, waiting for transfers between devices, body(): lax.all_gather(teacher_proto, 'dp', axis=0, tiled=True)  53.6 us
    psum x1, waiting for transfers between devices, body(): along, squares = lax.psum((along_part, squares_part), 'dp')  52 us
    dot_general x5, matrix products, block_expo(): jnp.dot(rows, student_unit, precision=highest, preferred_element_type=jnp...  46.2 us
    dot_general x5, matrix products, grad_block(): jnp.dot(dscore, student_unit.T, precision=highest, preferred_element_type...  39.8 us
    psum x1, waiting for transfers between devices, body(): feature_unit = lax.psum(feature_part, 'proto')  31.2 us
  transfers between devices with their start and end apart: 5, of which 4 were waited for; matrix products, arithmetic and copies ran while one was open for 3% of the time, Pallas kernels for 0%

commit v1 on v0

v1 whole, which is shorter than its diff:
```python
import jax
import jax.numpy as jnp
from jax import lax
from jax.sharding import PartitionSpec as P

CROPS = 10
GLOBAL_CROPS = 2
ITERS = 3
WARM_STEPS = 12500
TOTAL_STEPS = 625000


student_temp = 0.1
loss_scale = 16777216.0
norm_eps = 1e-06
square_eps = 1e-06
rate_peak = 0.05
weight_decay = 0.04
momentum_base = 0.994
highest = lax.Precision.HIGHEST


def plan(step):
    value = step[0].astype(jnp.float32)
    ramp = jnp.minimum(1.0, value / WARM_STEPS)
    rate = rate_peak * (0.25 + 0.75 * ramp)
    teacher_temp = 0.04 + 0.03 * ramp
    momentum = 1.0 - (1.0 - momentum_base) * (jnp.cos(jnp.pi * value / TOTAL_STEPS) + 1.0) * 0.5
    return (rate, teacher_temp, momentum)


def unit_rows(values):
    norm = jnp.sqrt(jnp.sum(values * values, axis=1, keepdims=True) + norm_eps)
    return (values / norm, norm)


def unit_columns(values):
    norm = jnp.sqrt(jnp.sum(values * values, axis=0, keepdims=True) + norm_eps)
    return (values / norm, norm)


def dot(left, right, dims):
    return lax.dot_general(
        left, right, (dims, ((), ())), precision=highest, preferred_element_type=jnp.float32
    )


def body(student_feats, teacher_feats, student_proto, teacher_proto, crops, step):
    rate, teacher_temp, momentum = plan(step)
    parts = lax.axis_size("dp")
    t_unit, t_norm = unit_rows(teacher_feats)
    s_unit, s_norm = unit_rows(student_feats)
    crop_rows, width = s_unit.shape
    teach_rows = t_unit.shape[0]
    own_rows, columns = student_proto.shape
    share = columns // parts
    images = teach_rows // GLOBAL_CROPS * parts
    pair_total = GLOBAL_CROPS * (GLOBAL_CROPS - 1) + (CROPS - GLOBAL_CROPS) * GLOBAL_CROPS
    coef = loss_scale / (pair_total * images * student_temp)
    teach_iota = lax.broadcasted_iota(jnp.int32, (1, teach_rows), 1)
    same = crops[:, 0:1] == teach_iota // GLOBAL_CROPS
    other = crops[:, 1:2] != teach_iota % GLOBAL_CROPS
    pairs = jnp.where(same & other, 1.0, 0.0).astype(jnp.float32)
    count = jnp.sum(pairs, axis=1, keepdims=True)
    mixed = dot(pairs, s_unit, ((0,), (0,)))
    count_rows = jnp.pad(count.reshape(1, crop_rows), ((0, 0), (0, -crop_rows % width)))
    count_rows = count_rows.reshape(-1, width)
    packed = jnp.concatenate([s_unit, t_unit, mixed, count_rows], axis=0)
    packed = lax.all_gather(packed, "dp", axis=0, tiled=False)
    protos = jnp.stack([student_proto, teacher_proto])
    protos = lax.all_to_all(protos, "dp", split_axis=2, concat_axis=1, tiled=True)
    one, two = crop_rows, crop_rows + teach_rows
    three = two + teach_rows
    all_s = packed[:, :one].reshape(parts * crop_rows, width)
    all_t = packed[:, one:two].reshape(parts * teach_rows, width)
    all_mixed = packed[:, two:three].reshape(parts * teach_rows, width)
    all_count = packed[:, three:].reshape(parts, -1)[:, :crop_rows].reshape(-1, 1)
    student_cols = protos[0]
    student_unit, student_norm = unit_columns(student_cols)
    teacher_unit, teacher_norm = unit_columns(protos[1])
    both = ("dp", "proto")
    assign = jnp.exp(dot(all_t, teacher_unit, ((1,), (0,))) / teacher_temp)
    expo = jnp.exp(dot(all_s, student_unit, ((1,), (0,))) / student_temp)
    total = jnp.sum(expo, axis=1)
    for turn in range(ITERS):
        assign = assign / jnp.sum(assign, axis=0, keepdims=True)
        row = jnp.sum(assign, axis=1)
        if turn == 0:
            row, total = lax.psum((row, total), both)
        else:
            row = lax.psum(row, both)
        assign = assign / row[:, None]
    total = total[:, None]
    back = dot(expo, student_unit, ((1,), (1,))).reshape(parts, crop_rows, width)
    back_target = dot(assign, student_unit, ((1,), (1,))).reshape(parts, teach_rows, width)
    sums = lax.psum_scatter(
        jnp.concatenate([back, back_target], axis=1), "dp", scatter_dimension=0, tiled=False
    )
    sums = lax.psum(sums, "proto")
    own_total = lax.dynamic_slice_in_dim(total, lax.axis_index("dp") * crop_rows, crop_rows, 0)
    feature_unit = coef * (
        count * (sums[:crop_rows] / own_total) - dot(pairs, sums[crop_rows:], ((1,), (0,)))
    )
    feature_grad = (
        feature_unit - s_unit * jnp.sum(s_unit * feature_unit, axis=1, keepdims=True)
    ) / s_norm
    grad_unit = coef * (
        dot(all_s * (all_count / total), expo, ((0,), (0,)))
        - dot(all_mixed, assign, ((0,), (0,)))
    )
    along = jnp.sum(student_unit * grad_unit, axis=0, keepdims=True)
    proto_grad = (grad_unit - student_unit * along) / student_norm
    square = jnp.mean(proto_grad * proto_grad, axis=0, keepdims=True)
    direction = proto_grad / jnp.sqrt(square + square_eps)
    student_next = student_cols - rate * (direction + weight_decay * student_cols)
    student_next = lax.all_to_all(
        student_next, "dp", split_axis=0, concat_axis=1, tiled=True
    )
    teacher_next = momentum * teacher_proto + (1.0 - momentum) * student_next
    return (student_next, teacher_next, feature_grad)


def solution(mesh):
    in_specs = (
        P("dp", None),
        P("dp", None),
        P("dp", "proto"),
        P("dp", "proto"),
        P("dp", None),
        P(),
    )
    out_specs = (P("dp", "proto"), P("dp", "proto"), P("dp", None))
    return jax.shard_map(body, mesh=mesh, in_specs=in_specs, out_specs=out_specs, check_vma=False)
```

time: 521 us -> 333 us (0.64)
  matrix products: 158 us -> 27.2 us
  waiting for transfers between devices: 212 us -> 91 us
  local copies, waits for them, and re-layouts: 4.04 us -> 48 us
  blocking collectives: 99.8 us -> 120 us
  starting transfers between devices: 0.19 us -> 9.19 us
  other arithmetic: 30.3 us -> 21.7 us
    dot_general x21 -> x8, matrix products: 158 us -> 27.2 us  [dot(): lax.dot_general(left, right, (dims, ((), ())), precision=highest, preferr...]
    reduce_scatter x1, waiting for transfers between devices: 73.6 us -> 9.52 us  [body(): lax.psum_scatter(jnp.concatenate([back, back_target], axis=1), 'dp', scat...]
    all_gather x2 -> x1, waiting for transfers between devices: 53.6 us -> 0.01 us  [body(): packed = lax.all_gather(packed, 'dp', axis=0, tiled=False)]
    psum x2 -> x1, waiting for transfers between devices: 83.3 us -> 36.1 us  [body(): sums = lax.psum(sums, 'proto')]
    all_to_all x0 -> x2, waiting for transfers between devices: none -> 45.4 us  [the longest x1 25.9 us: body(): lax.all_to_all(protos, 'dp', split_axis=2, concat_axis=1, tiled=True)]
    unnamed x12 -> x29, local copies, waits for them, and re-layouts: 3.05 us -> 25.7 us
    psum x6 -> x3, blocking collectives: 99.8 us -> 120 us  [the longest x2 80.4 us: body(): row = lax.psum(row, both)]
    all_to_all x0 -> x3, local copies, waits for them, and re-layouts: none -> 10.8 us  [the longest x2 10.7 us: body(): lax.all_to_all(protos, 'dp', split_axis=2, concat_axis=1, tiled=True)]
  transfers between devices with their start and end apart: 5 -> 5, of which waited for: 4 -> 4; matrix products, arithmetic and copies ran while one was open for 3% -> 19% of each run, Pallas kernels for 0% -> 0%
where the time goes in v1:
time: 333 us; the launch traced here: 332 us
  blocking collectives  120 us (36%)
  waiting for transfers between devices  91 us (27%)
  local copies, waits for them, and re-layouts  48 us (14%)
  matrix products  27.2 us (8%)
  other arithmetic  21.7 us (7%)
  between operations  14.8 us (4%)
  starting transfers between devices  9.19 us (3%)
    psum x2, blocking collectives, body(): row = lax.psum(row, both)  80.4 us
    psum x1, blocking collectives, body(): row, total = lax.psum((row, total), both)  39.5 us
    psum x1, waiting for transfers between devices, body(): sums = lax.psum(sums, 'proto')  36.1 us
    dot_general x8, matrix products, dot(): lax.dot_general(left, right, (dims, ((), ())), precision=highest, preferr...  27.2 us
    all_to_all x1, waiting for transfers between devices, body(): lax.all_to_all(protos, 'dp', split_axis=2, concat_axis=1, tiled=True)  25.9 us
    unnamed x29, local copies, waits for them, and re-layouts  25.7 us
    all_to_all x1, waiting for transfers between devices, body(): lax.all_to_all(student_next, 'dp', split_axis=0, concat_axis=1, tiled=True)  19.4 us
    all_to_all x2, local copies, waits for them, and re-layouts, body(): lax.all_to_all(protos, 'dp', split_axis=2, concat_axis=1, tiled=True)  10.7 us
  transfers between devices with their start and end apart: 5, of which 4 were waited for; matrix products, arithmetic and copies ran while one was open for 19% of the time, Pallas kernels for 0%

profile of v1, /device:TPU:0, one launch (start us, length us, event | category | flops | bytes accessed | tf_op | source)
XLA Modules:
  0.0 331.7 jit_solution(8081224339155919855)
XLA Ops:
  7.2 0.9 multiply_reduce_fusion.6
  8.2 1.0 multiply_reduce_fusion.5
  9.2 0.8 fusion.41
  10.0 0.8 broadcast_divide_fusion.2
  10.8 1.0 broadcast_divide_fusion.1
  12.0 0.2 fusion.21
  12.2 0.3 copy-done.10
  12.5 0.7 fusion.18
  13.3 1.4 pad_maximum_fusion
  14.6 7.9 %copy.18 = f32[2,32,8192]{1,0,2:T(2,128)} copy(f32[2,32,8192]{2,1,0:T(8,128)S(1)} %pad_maximum_fusion) | data formatting | bytes 4194304 | tf_op jit(solution)/shard_map/stack | solution.py:70
  22.5 11.4 %reshape.188 = f32[8,1,65536]{2,1,0:T(1,128)} reshape(f32[8192,2,32]{2,1,0:T(2,128)} %bitcast.63) | data formatting | bytes 4194304
  33.9 5.2 %all-to-all-start = ((f32[8,1,65536]{2,1,0:T(1,128)}), f32[8,1,65536]{2,1,0:T(1,128)S(1)}, u32[]{:S(2)}, u32[]{:S(2)}) async-start(f32[8,1,65536]{2,1,0:T(1,128)} %reshape.188), calls=%async_computation | async-start | bytes 4194304 | tf_op jit(solution)/shard_map/all_to_all | solution.py:71
  39.8 25.9 %all-to-all-done = f32[8,1,65536]{2,1,0:T(1,128)S(1)} async-done(((f32[8,1,65536]{2,1,0:T(1,128)}), f32[8,1,65536]{2,1,0:T(1,128)S(1)}, u32[]{:S(2)}, u32[]{:S(2)}) %all-to-all-start) | async-done | bytes 2097184 | tf_op jit(solution)/shard_map/all_to_all | solution.py:71
  65.8 1.3 copy-done.5
  67.1 0.5 broadcast.136
  67.6 7.2 %reduce.2 = f32[8,65536]{1,0:T(8,128)S(1)} reduce(f32[8,1,65536]{2,1,0:T(1,128)} %copy-done.5, f32[]{:T(128)} %broadcast.136), dimensions={1}, to_apply=%all_to_all.25.reduce_sub_computation | reduce | bytes 4194308 | tf_op jit(solution)/shard_map/all_to_all | solution.py:71
  74.8 10.3 %reshape.189 = f32[8192,2,32]{2,1,0:T(2,128)} reshape(f32[8,65536]{1,0:T(8,128)S(1)} %reduce.2) | data formatting | bytes 4194304
  85.1 10.2 %copy.19 = f32[2,32,8,1024]{3,1,2,0:T(8,128)S(1)} copy(f32[2,32,8,1024]{1,0,3,2:T(2,128)} %bitcast.64) | data formatting | bytes 4194304 | tf_op jit(solution)/shard_map/all_to_all | solution.py:71
  95.5 1.7 broadcast_divide_fusion
  97.2 0.8 slice.48
  98.1 1.8 fusion.40
  99.9 2.3 fusion.42
  102.4 39.5 %psum.36 = f32[256]{0:T(256)S(1)} all-reduce(f32[256]{0:T(256)S(1)} %divide_reduce_fusion), channel_id=1, replica_groups=mesh['dp'=8,'proto'=4] {'dp','proto'}, use_global_device_ids=true, to_apply=%region_9.10 | all-reduce | flops 256 | bytes 2048 | tf_op jit(solution)/shard_map/psum | solution.py:89
  141.9 0.2 fusion.13
  142.2 0.3 fusion.14
  142.5 40.2 %psum.37 = f32[256]{0:T(256)S(1)} all-reduce(f32[256]{0:T(256)S(1)} %fusion.14), channel_id=1, replica_groups=mesh['dp'=8,'proto'=4] {'dp','proto'}, use_global_device_ids=true, to_apply=%region_12.13 | all-reduce | flops 256 | bytes 2048 | tf_op jit(solution)/shard_map/psum | solution.py:91
  182.7 0.3 fusion.15
  183.0 0.4 fusion.16
  183.4 0.8 copy-done.9
  184.6 6.6 %fusion.43 = (f32[1280]{0:T(1024)S(1)}, f32[1280,1024]{1,0:T(8,128)}) fusion(f32[1280,256]{1,0:T(8,128)S(1)} %bitcast.70, f32[256,1024]{1,0:T(8,128)S(1)} %bitcast.67), kind=kOutput, calls=%fused_computation.85 | convolution fusion | flops 4029152000 | bytes 7607296 | tf_op jit(solution)/shard_map/dot_general | solution.py:43
  191.1 40.2 %all-reduce.1 = (f32[256]{0:T(256)S(1)}, f32[1280]{0:T(1024)S(1)}) all-reduce(f32[256]{0:T(256)S(1)} %fusion.16, f32[1280]{0:T(1024)S(1)} %get-tuple-element.16), channel_id=1, replica_groups=mesh['dp'=8,'proto'=4] {'dp','proto'}, use_global_device_ids=true, to_apply=%region_15.16 | all-reduce | flops 1536 | bytes 12288 | tf_op jit(solution)/shard_map/psum | solution.py:91
  231.3 0.4 fusion.10
  231.7 1.0 copy-done.3
  232.7 1.0 fusion.46
  233.7 6.3 %fusion.45 = f32[8,160,256]{2,1,0:T(8,128)S(1)} fusion(f32[8,160,1024]{2,1,0:T(8,128)} %bitcast.62, f32[256,1024,1]{1,0,2:T(8,128)S(1)} %bitcast.69), kind=kOutput, calls=%fused_computation.87 | convolution fusion | flops 4026531840 | bytes 7602176 | tf_op jit(solution)/shard_map/dot_general | solution.py:43
  240.0 1.3 pad_maximum_fusion.1
  241.4 0.3 copy-done.4
  241.6 2.1 fusion.44
  243.7 7.2 %multiply_reduce_fusion.1 = (f32[1024]{0:T(1024)S(1)}, f32[256,1024]{1,0:T(8,128)S(1)}) fusion(f32[1024]{0:T(1024)S(1)} %add_sqrt_fusion.1, f32[1,8,32,1024]{3,2,1,0:T(8,128)S(1)} %get-tuple-element.9, f32[256,1024]{1,0:T(8,128)S(1)} %fusion.44, f32[1280,1024]{1,0:T(8,128)} %get-tuple-element.17, f32[1280,256]{1,0:T(8,128)S(1)} %bitcast.71, f32[1280]{0:T(1024)S(1)} %div.165), kind=kOutput, calls=%fused_computation.27 | convolution fusion | flops 4028169216 | bytes 9712640 | tf_op jit(solution)/shard_map/dot_general | solution.py:43
  251.0 0.2 multiply_reduce_fusion
  251.2 1.3 bitcast_subtract_fusion
  252.5 3.9 %all-to-all-start.1 = ((f32[8,32,1024]{2,1,0:T(8,128)}), f32[8,32,1024]{2,1,0:T(8,128)S(1)}, u32[]{:S(2)}, u32[]{:S(2)}) async-start(f32[8,32,1024]{2,1,0:T(8,128)} %bitcast.16), calls=%async_computation.1 | async-start | bytes 2097152 | tf_op jit(solution)/shard_map/all_to_all | solution.py:116
  256.6 19.4 %all-to-all-done.1 = f32[8,32,1024]{2,1,0:T(8,128)S(1)} async-done(((f32[8,32,1024]{2,1,0:T(8,128)}), f32[8,32,1024]{2,1,0:T(8,128)S(1)}, u32[]{:S(2)}, u32[]{:S(2)}) %all-to-all-start.1) | async-done | bytes 1048608 | tf_op jit(solution)/shard_map/all_to_all | solution.py:116
  276.2 9.5 %reduce-scatter.2.cloned.1.call-done = f32[1,192,256]{2,1,0:T(8,128)} async-done(((f32[8,192,256]{2,1,0:T(8,128)}), f32[1,192,256]{2,1,0:T(8,128)}) %reduce-scatter.2.cloned.1.call-update) | async-done | bytes 196624 | tf_op jit(solution)/shard_map/reduce_scatter | solution.py:96
  285.7 1.1 multiply_add_fusion
  286.8 36.1 %all-reduce.4.cloned.1.call-done = f32[192,256]{1,0:T(8,128)} async-done(((f32[192,256]{1,0:T(8,128)}), f32[192,256]{1,0:T(8,128)}) %all-reduce.4.cloned.1.call-update) | async-done | bytes 196624 | tf_op jit(solution)/shard_map/psum | solution.py:99
  322.9 1.5 multiply_reduce_fusion.4
  324.4 0.8 subtract_divide_fusion
  (43 shorter events, 1.3 us)
Async XLA Ops:
  7.2 6.1 %copy-start.7 = (f32[32,8192]{1,0:T(8,128)S(1)}, f32[32,8192]{1,0:T(8,128)}, u32[]{:S(2)}) copy-start(f32[32,8192]{1,0:T(8,128)} %param.9) | copy-start | bytes 3145732
  7.2 90.0 %all-gather.4.cloned.1.call-start = ((), (), s32[]{:S(2)}) async-start(), calls=%async_computation.5 | async-start | bytes 2138112 | tf_op jit(solution)/shard_map/all_gather | solution.py:69
  11.9 0.7 copy-start.10
  33.9 31.8 %all-to-all-start = ((f32[8,1,65536]{2,1,0:T(1,128)}), f32[8,1,65536]{2,1,0:T(1,128)S(1)}, u32[]{:S(2)}, u32[]{:S(2)}) async-start(f32[8,1,65536]{2,1,0:T(1,128)} %reshape.188), calls=%async_computation | async-start | bytes 4194304 | tf_op jit(solution)/shard_map/all_to_all | solution.py:71
  39.1 246.6 %reduce-scatter.2.cloned.1.call-start = ((), (), s32[]{:S(2)}) async-start(), calls=%async_computation.3 | async-start | bytes 1769472 | tf_op jit(solution)/shard_map/reduce_scatter | solution.py:96
  65.8 1.4 copy-start.5
  182.7 1.5 copy-start.9
  183.0 1.6 copy-start
  184.3 6.8 %copy-start.1 = (f32[8,160,256]{2,1,0:T(8,128)}, f32[8,160,256]{2,1,0:T(8,128)S(1)}, u32[]{:S(2)}) copy-start(f32[8,160,256]{2,1,0:T(8,128)S(1)} %slice.47) | copy-start | bytes 3932164
  231.7 1.0 copy-start.3
  240.0 1.7 copy-start.4
  241.3 2.4 copy-start.2
  252.5 33.2 %copy-start.8 = (f32[32,8192]{1,0:T(8,128)S(1)}, f32[32,8192]{1,0:T(8,128)}, u32[]{:S(2)}) copy-start(f32[32,8192]{1,0:T(8,128)} %param.9) | copy-start | bytes 3145732
  252.5 23.5 %all-to-all-start.1 = ((f32[8,32,1024]{2,1,0:T(8,128)}), f32[8,32,1024]{2,1,0:T(8,128)S(1)}, u32[]{:S(2)}, u32[]{:S(2)}) async-start(f32[8,32,1024]{2,1,0:T(8,128)} %bitcast.16), calls=%async_computation.1 | async-start | bytes 2097152 | tf_op jit(solution)/shard_map/all_to_all | solution.py:116
  256.4 66.5 %all-reduce.4.cloned.1.call-start = ((), (), s32[]{:S(2)}) async-start(), calls=%async_computation.4 | async-start | bytes 393216 | tf_op jit(solution)/shard_map/psum | solution.py:99
  276.2 48.2 %copy-start.6 = (f32[8,4,8,1024]{3,2,0,1:T(8,128)}, f32[8,4,8,1024]{3,2,0,1:T(8,128)S(1)}, u32[]{:S(2)}) copy-start(f32[8,4,8,1024]{3,2,0,1:T(8,128)S(1)} %copy.22) | copy-start | bytes 3145732
  276.2 46.7 %copy-start.11 = (f32[160,256]{1,0:T(8,128)S(1)}, f32[160,256]{1,0:T(8,128)}, u32[]{:S(2)}) copy-start(f32[160,256]{1,0:T(8,128)} %copy-done.10) | copy-start | bytes 491524
  285.7 38.6 %copy-start.12 = (f32[160,256]{1,0:T(8,128)S(1)}, f32[160,256]{1,0:T(8,128)}, u32[]{:S(2)}) copy-start(f32[160,256]{1,0:T(8,128)} %param.6) | copy-start | bytes 491524
Sparse Core Ops, SparseCore 0:
  13.4 29.7 all-gather.3
  241.5 44.1 reduce-scatter.1
  288.0 34.8 all-reduce.3

commit v2 on v1

v2 whole, which is shorter than its diff:
```python
import functools

import jax
import jax.numpy as jnp
from jax import lax
from jax.experimental import pallas as pl
from jax.experimental.pallas import tpu as pltpu
from jax.sharding import PartitionSpec as P

CROPS = 10
GLOBAL_CROPS = 2
ITERS = 3
WARM_STEPS = 12500
TOTAL_STEPS = 625000


student_temp = 0.1
loss_scale = 16777216.0
norm_eps = 1e-06
square_eps = 1e-06
rate_peak = 0.05
weight_decay = 0.04
momentum_base = 0.994
highest = lax.Precision.HIGHEST


def plan(step):
    value = step[0].astype(jnp.float32)
    ramp = jnp.minimum(1.0, value / WARM_STEPS)
    rate = rate_peak * (0.25 + 0.75 * ramp)
    teacher_temp = 0.04 + 0.03 * ramp
    momentum = 1.0 - (1.0 - momentum_base) * (jnp.cos(jnp.pi * value / TOTAL_STEPS) + 1.0) * 0.5
    return (rate, teacher_temp, momentum)


NN = (((1,), (0,)), ((), ()))
NT = (((1,), (1,)), ((), ()))
MESH = pl.DeviceIdType.MESH
LANES = 128
SUBLANES = 8
f32 = jnp.float32
bf16 = jnp.bfloat16


def dot(left, right, dims):
    return lax.dot_general(left, right, dims, precision=highest, preferred_element_type=f32)


def split(values):
    high = values.astype(bf16)
    return high, (values - high.astype(f32)).astype(bf16)


def dot3(left, right, dims):
    def one(a, b):
        return lax.dot_general(a, b, dims, preferred_element_type=f32)

    return one(left[0], right[0]) + (one(left[0], right[1]) + one(left[1], right[0]))


def fold(values):
    rows, columns = values.shape
    return jnp.sum(values.reshape(rows // SUBLANES, SUBLANES, columns), axis=0)


def kernel(
    parts, groups, coef,
    plan_ref, sf_ref, tf_ref, sp_ref, tp_ref, crops_ref, crops_t_ref,
    snext_ref, tnext_ref, fgrad_ref,
    sp_in, tp_in, s_in, t_in, own_s, own_t, unit_hi, unit_lo, expo_hi, expo_lo,
    lane_part, inv_total, weighted, assign, row_dp, row_pr, tot_dp, tot_pr,
    f_send, f_dp, f_part, f_pr, f_sum, g_send, g_dp, g_part, g_pr, moved, landed,
    dp_send, dp_recv, f_ssem, f_rsem, pr_send, pr_recv, back_send, back_recv, local_sem,
):
    me, mine = lax.axis_index("dp"), lax.axis_index("proto")
    crop_rows, width = sf_ref.shape
    teach_rows = tf_ref.shape[0]
    own_rows, columns = sp_ref.shape
    share = columns // parts
    rate, temp, momentum = plan_ref[0], plan_ref[1], plan_ref[2]
    dp_peers = [lax.rem(me + hop, parts) for hop in range(1, parts)]
    pr_peers = [lax.rem(mine + hop, groups) for hop in range(1, groups)]
    barrier = pltpu.get_barrier_semaphore()
    for peer in dp_peers:
        pl.semaphore_signal(barrier, inc=1, device_id={"dp": peer}, device_id_type=MESH)
    for peer in pr_peers:
        pl.semaphore_signal(barrier, inc=1, device_id={"proto": peer}, device_id_type=MESH)

    t_values = tf_ref[...]
    own_t[...] = t_values / jnp.sqrt(jnp.sum(t_values * t_values, axis=1, keepdims=True) + norm_eps)
    s_values = sf_ref[...]
    s_norm = jnp.sqrt(jnp.sum(s_values * s_values, axis=1, keepdims=True) + norm_eps)
    s_unit = s_values / s_norm
    teach = lax.broadcasted_iota(jnp.int32, (teach_rows, crop_rows), 0)
    same = crops_t_ref[0:1, :] == teach // GLOBAL_CROPS
    other = crops_t_ref[1:2, :] != teach % GLOBAL_CROPS
    pairs_t = jnp.where(same & other, 1.0, 0.0).astype(f32)
    mixed_at, count_at = crop_rows, crop_rows + teach_rows
    own_s[0:crop_rows, :] = s_unit
    own_s[mixed_at:count_at, :] = dot(pairs_t, s_unit, NN)
    own_s[count_at:, :] = jnp.zeros((SUBLANES, width), f32)
    own_s[count_at:, 0:crop_rows] = jnp.broadcast_to(
        jnp.sum(pairs_t, axis=0, keepdims=True), (SUBLANES, crop_rows)
    )
    pl.semaphore_wait(barrier, parts - 1 + groups - 1)

    def remote(kind, hop, axis, peer, src, dst, ssem, rsem):
        return pltpu.make_async_remote_copy(
            src_ref=src, dst_ref=dst, send_sem=ssem.at[kind, hop], recv_sem=rsem.at[kind, hop],
            device_id={axis: peer}, device_id_type=MESH,
        )

    def cols(which):
        return pl.ds(pl.multiple_of(which * share, share), share)

    def rows(which, size):
        return pl.ds(pl.multiple_of(which * size, size), size)

    own_block = rows(me, own_rows)
    teacher_moves, student_moves, sends = [], [], []
    for hop, peer in enumerate(dp_peers):
        teacher_moves.append(remote(0, hop, "dp", peer, tp_ref.at[:, cols(peer)], tp_in.at[own_block, :], dp_send, dp_recv))
        teacher_moves.append(remote(1, hop, "dp", peer, own_t, t_in.at[rows(me, teach_rows), :], dp_send, dp_recv))
        student_moves.append(remote(2, hop, "dp", peer, sp_ref.at[:, cols(peer)], sp_in.at[own_block, :], dp_send, dp_recv))
        student_moves.append(remote(3, hop, "dp", peer, own_s, s_in.at[me], dp_send, dp_recv))
    for move in teacher_moves + student_moves:
        move.start()
        sends.append(move)
    local_moves = [
        pltpu.make_async_copy(tp_ref.at[:, cols(me)], tp_in.at[own_block, :], local_sem.at[0]),
        pltpu.make_async_copy(sp_ref.at[:, cols(me)], sp_in.at[own_block, :], local_sem.at[1]),
    ]
    for move in local_moves:
        move.start()
    t_in[rows(me, teach_rows), :] = own_t[...]
    s_in[me] = own_s[...]
    for move in local_moves:
        move.wait()

    def exchange(values, first, second, kind):
        first[me] = values
        moves = [
            remote(kind, hop, "dp", peer, first.at[me], first.at[me], dp_send, dp_recv)
            for hop, peer in enumerate(dp_peers)
        ]
        return spread(moves, first, second, kind)

    def spread(moves, first, second, kind):
        for move in moves:
            move.start()
            sends.append(move)

        def finish():
            for move in moves:
                move.wait_recv()
            second[mine] = jnp.sum(first[...], axis=0)
            later = [
                remote(kind, hop, "proto", peer, second.at[mine], second.at[mine], pr_send, pr_recv)
                for hop, peer in enumerate(pr_peers)
            ]
            for move in later:
                move.start()
                sends.append(move)

            def last():
                for move in later:
                    move.wait_recv()
                return jnp.sum(second[...], axis=0)

            return last

        return finish

    for move in teacher_moves:
        move.wait_recv()
    teacher_cols = tp_in[...]
    teacher_norm = jnp.sqrt(jnp.sum(teacher_cols * teacher_cols, axis=0, keepdims=True) + norm_eps)
    assign[...] = jnp.exp(dot((teacher_cols / teacher_norm).T, t_in[...], NT) / temp)
    for turn in range(ITERS):
        values = assign[...]
        values = values / jnp.sum(values, axis=1, keepdims=True)
        total = exchange(fold(values), row_dp.at[turn], row_pr.at[turn], 4 + turn)()()
        assign[...] = values / jnp.sum(total, axis=0, keepdims=True)

    for move in student_moves:
        move.wait_recv()
    student_cols = sp_in[...]
    student_norm = jnp.sqrt(jnp.sum(student_cols * student_cols, axis=0, keepdims=True) + norm_eps)
    high, low = split(student_cols / student_norm)
    unit_hi[...] = high
    unit_lo[...] = low

    def f_move(step, block):
        return remote(0, step, "dp", block, f_send.at[block], f_dp.at[me], f_ssem, f_rsem)

    def crop_block(step, carry):
        block = lax.rem(me + 1 + step, parts)
        at = rows(block, crop_rows)
        unit = (unit_hi[...], unit_lo[...])
        expo = jnp.exp(dot3(split(s_in[block, 0:crop_rows, :]), unit, NN) / student_temp)
        part = expo[:, 0:LANES]
        for lane in range(1, share // LANES):
            part = part + expo[:, lane * LANES:(lane + 1) * LANES]
        lane_part[at, :] = part
        pieces = split(expo)
        expo_hi[at, :] = pieces[0]
        expo_lo[at, :] = pieces[1]
        f_send[block] = dot3(pieces, unit, NT)

        @pl.when(step < parts - 1)
        def _():
            f_move(step, block).start()

        return carry

    lax.fori_loop(0, parts, crop_block, 0)
    finish = exchange(fold(lane_part[...].T), tot_dp, tot_pr, 4 + ITERS)

    g_send[...] = dot3((unit_hi[...], unit_lo[...]), split(assign[...]), NN).T
    g_moves = [
        remote(5 + ITERS, hop, "dp", peer, g_send.at[rows(peer, teach_rows), :], g_dp.at[me], dp_send, dp_recv)
        for hop, peer in enumerate(dp_peers)
    ]
    for move in g_moves:
        move.start()
        sends.append(move)
    g_dp[me] = g_send[rows(me, teach_rows), :]
    last = finish()
    f_dp[me] = f_send[me]
    mixed = s_in[:, mixed_at:count_at, :].reshape(parts * teach_rows, width)
    mixed_t = split(mixed.T)
    total = jnp.sum(last(), axis=0, keepdims=True)
    inv_total[...] = jnp.broadcast_to(1.0 / total, (LANES, parts * crop_rows)).T
    for block in range(parts):
        at = slice(block * crop_rows, (block + 1) * crop_rows)
        count = jnp.broadcast_to(s_in[block, count_at:count_at + 1, :], (LANES, width)).T
        weight = count[0:crop_rows, :] * inv_total[at, :]
        weighted[at, :] = s_in[block, 0:crop_rows, :] * jnp.concatenate([weight] * (width // LANES), axis=1)
    weighted_t = split(weighted[...].T)

    chunk = share // 2
    back_moves = []
    for piece in range(2):
        at = slice(piece * chunk, (piece + 1) * chunk)
        grad = coef * (
            dot3(weighted_t, (expo_hi[:, at], expo_lo[:, at]), NN)
            - dot3(mixed_t, split(assign[at, :]), NT)
        )
        now = sp_in[:, at]
        norm = jnp.sqrt(jnp.sum(now * now, axis=0, keepdims=True) + norm_eps)
        unit = now / norm
        proto_grad = (grad - unit * jnp.sum(unit * grad, axis=0, keepdims=True)) / norm
        square = jnp.sum(proto_grad * proto_grad, axis=0, keepdims=True) / width
        direction = proto_grad / jnp.sqrt(square + square_eps)
        moved[:, at] = now - rate * (direction + weight_decay * now)
        place = pl.ds(pl.multiple_of(me * share + piece * chunk, chunk), chunk)
        for hop, peer in enumerate(dp_peers):
            move = remote(piece, hop, "dp", peer, moved.at[rows(peer, own_rows), at], landed.at[:, place], back_send, back_recv)
            move.start()
            back_moves.append(move)
        landed[:, place] = moved[own_block, at]

    f_moves = [f_move(step, peer) for step, peer in enumerate(dp_peers)]
    for move in f_moves:
        move.wait_recv()
    f_part[...] = jnp.sum(f_dp[...], axis=0)
    for move in g_moves:
        move.wait_recv()
    g_pr[mine] = jnp.sum(g_dp[...], axis=0)
    f_pr[mine] = f_part[...]
    z_moves = []
    for hop, peer in enumerate(pr_peers):
        z_moves.append(remote(5 + ITERS, hop, "proto", peer, f_pr.at[mine], f_pr.at[mine], pr_send, pr_recv))
        z_moves.append(remote(6 + ITERS, hop, "proto", peer, g_pr.at[mine], g_pr.at[mine], pr_send, pr_recv))
    for move in z_moves:
        move.start()
        sends.append(move)
    for move in z_moves:
        move.wait_recv()
    teach = lax.broadcasted_iota(jnp.int32, (crop_rows, teach_rows), 1)
    same = crops_ref[:, 0:1] == teach // GLOBAL_CROPS
    other = crops_ref[:, 1:2] != teach % GLOBAL_CROPS
    pairs = jnp.where(same & other, 1.0, 0.0).astype(f32)
    count = jnp.sum(pairs, axis=1, keepdims=True)
    inverse = jnp.concatenate([inv_total[rows(me, crop_rows), :]] * (width // LANES), axis=1)
    feature_unit = coef * (
        count * (jnp.sum(f_pr[...], axis=0) * inverse) - dot(pairs, jnp.sum(g_pr[...], axis=0), NN)
    )
    s_values = sf_ref[...]
    s_norm = jnp.sqrt(jnp.sum(s_values * s_values, axis=1, keepdims=True) + norm_eps)
    s_unit = s_values / s_norm
    fgrad_ref[...] = (
        feature_unit - s_unit * jnp.sum(s_unit * feature_unit, axis=1, keepdims=True)
    ) / s_norm

    for move in back_moves:
        move.wait_recv()
    student_next = landed[...]
    snext_ref[...] = student_next
    tnext_ref[...] = momentum * tp_ref[...] + (1.0 - momentum) * student_next
    for move in sends + f_moves + back_moves:
        move.wait_send()


def body(student_feats, teacher_feats, student_proto, teacher_proto, crops, step):
    parts, groups = lax.axis_size("dp"), lax.axis_size("proto")
    crop_rows, width = student_feats.shape
    teach_rows = teacher_feats.shape[0]
    own_rows, columns = student_proto.shape
    share = columns // parts
    images = teach_rows // GLOBAL_CROPS * parts
    pair_total = GLOBAL_CROPS * (GLOBAL_CROPS - 1) + (CROPS - GLOBAL_CROPS) * GLOBAL_CROPS
    coef = loss_scale / (pair_total * images * student_temp)
    all_s, all_t = parts * crop_rows, parts * teach_rows
    packed = crop_rows + teach_rows + SUBLANES
    kinds = 7 + ITERS

    def vmem(*shape, dtype=f32):
        return pltpu.VMEM(shape, dtype)

    def sems(*shape):
        return pltpu.SemaphoreType.DMA(shape)

    whole = pl.BlockSpec(memory_space=pltpu.VMEM)
    shapes = [student_proto, teacher_proto, student_feats]
    return pl.pallas_call(
        functools.partial(kernel, parts, groups, coef),
        out_shape=[jax.ShapeDtypeStruct(one.shape, f32) for one in shapes],
        in_specs=[pl.BlockSpec(memory_space=pltpu.SMEM)] + [whole] * 6,
        out_specs=[whole] * 3,
        scratch_shapes=[
            vmem(width, share), vmem(width, share),
            vmem(parts, packed, width), vmem(all_t, width),
            vmem(packed, width), vmem(teach_rows, width),
            vmem(width, share, dtype=bf16), vmem(width, share, dtype=bf16),
            vmem(all_s, share, dtype=bf16), vmem(all_s, share, dtype=bf16),
            vmem(all_s, LANES), vmem(all_s, LANES), vmem(all_s, width),
            vmem(share, all_t),
            vmem(ITERS, parts, SUBLANES, all_t), vmem(ITERS, groups, SUBLANES, all_t),
            vmem(parts, SUBLANES, all_s), vmem(groups, SUBLANES, all_s),
            vmem(parts, crop_rows, width), vmem(parts, crop_rows, width),
            vmem(crop_rows, width), vmem(groups, crop_rows, width), vmem(crop_rows, width),
            vmem(all_t, width), vmem(parts, teach_rows, width),
            vmem(teach_rows, width), vmem(groups, teach_rows, width),
            vmem(width, share), vmem(own_rows, columns),
            sems(kinds, parts), sems(kinds, parts), sems(1, parts), sems(1, parts),
            sems(kinds, groups), sems(kinds, groups), sems(2, parts), sems(2, parts), sems(2),
        ],
        compiler_params=pltpu.CompilerParams(
            collective_id=0, has_side_effects=True, vmem_limit_bytes=56 * 1024 * 1024
        ),
    )(jnp.stack(plan(step)), student_feats, teacher_feats, student_proto, teacher_proto, crops, crops.T)


def solution(mesh):
    in_specs = (
        P("dp", None),
        P("dp", None),
        P("dp", "proto"),
        P("dp", "proto"),
        P("dp", None),
        P(),
    )
    out_specs = (P("dp", "proto"), P("dp", "proto"), P("dp", None))
    return jax.shard_map(body, mesh=mesh, in_specs=in_specs, out_specs=out_specs, check_vma=False)
```

time: 333 us -> 133 us (0.40)
  the two profiles are of different devices: /device:TPU:0 before, /device:TPU:26 now
where the time goes in v2:
time: 133 us
  Pallas kernels  126 us (95%)
  local copies, waits for them, and re-layouts  4.92 us (4%)
  between operations  1.39 us (1%)
    pallas_call x1, Pallas kernels, body(): pl.pallas_call(functools.partial(kernel, parts, groups, coef), out_shape=...  126 us
    unnamed x10, local copies, waits for them, and re-layouts  4.92 us

profile of v2, /device:TPU:26, one launch (start us, length us, event | category | flops | bytes accessed | tf_op | source)
XLA Modules:
  0.0 132.6 jit_solution(10028366152294875003)
XLA Ops:
  1.4 0.0 copy-start.2
  1.4 0.6 pad_maximum_fusion.plan_ref
  2.0 0.1 copy-done.2
  2.0 0.8 copy.9.crops_ref
  2.8 125.7 %shard_map.85 = (f32[32,8192]{1,0:T(8,128)}, f32[32,8192]{1,0:T(8,128)}, f32[160,256]{1,0:T(8,128)}) custom-call(f32[3]{0:T(128)} %pad_maximum_fusion.plan_ref, f32[160,256]{1,0:T(8,128)} %sf_ref.1, f32[32,256]{1,0:T(8,128)} %tf_ref.1, f32[32,8192]{1,0:T(8,128)} %sp_ref.1, f32[32,8192]{1,0:T(8,128)} %tp_ref.1, s32[160,2]{1,0:T(8,128)} %copy.9.crops_ref, ...), custom_call_target="tpu_custom_call" | custom-call | tf_op jit(solution)/shard_map/pallas_call | solution.py:326
  128.5 0.0 copy-start
  128.6 2.4 %copy.14 = f32[32,8192]{1,0:T(8,128)} copy(f32[32,8192]{1,0:T(8,128)} %get-tuple-element.6) | data formatting | bytes 2097152
  130.9 0.0 copy-done
  130.9 0.0 copy-start.1
  130.9 1.0 copy.15
  131.9 0.1 copy-done.1
  132.0 0.7 copy.16
Async XLA Ops:
  1.4 0.7 copy-start.2
  128.5 2.4 %copy-start = (f32[32,8192]{1,0:T(8,128)S(1)}, f32[32,8192]{1,0:T(8,128)}, u32[]{:S(2)}) copy-start(f32[32,8192]{1,0:T(8,128)} %get-tuple-element.7) | copy-start | bytes 3145732
  130.9 1.1 copy-start.1

commit v3 on v2

v3 whole, which is shorter than its diff:
```python
import functools

import jax
import jax.numpy as jnp
from jax import lax
from jax.experimental import pallas as pl
from jax.experimental.pallas import tpu as pltpu
from jax.sharding import PartitionSpec as P

CROPS = 10
GLOBAL_CROPS = 2
ITERS = 3
WARM_STEPS = 12500
TOTAL_STEPS = 625000


student_temp = 0.1
loss_scale = 16777216.0
norm_eps = 1e-06
square_eps = 1e-06
rate_peak = 0.05
weight_decay = 0.04
momentum_base = 0.994
highest = lax.Precision.HIGHEST


def plan(step):
    value = step[0].astype(jnp.float32)
    ramp = jnp.minimum(1.0, value / WARM_STEPS)
    rate = rate_peak * (0.25 + 0.75 * ramp)
    teacher_temp = 0.04 + 0.03 * ramp
    momentum = 1.0 - (1.0 - momentum_base) * (jnp.cos(jnp.pi * value / TOTAL_STEPS) + 1.0) * 0.5
    return (rate, teacher_temp, momentum)


NN = (((1,), (0,)), ((), ()))
NT = (((1,), (1,)), ((), ()))
MESH = pl.DeviceIdType.MESH
LANES = 128
SUBLANES = 8
f32 = jnp.float32
bf16 = jnp.bfloat16


def dot(left, right, dims):
    return lax.dot_general(left, right, dims, precision=highest, preferred_element_type=f32)


def split(values):
    high = values.astype(bf16)
    return high, (values - high.astype(f32)).astype(bf16)


def dot3(left, right, dims):
    def one(a, b):
        return lax.dot_general(a, b, dims, preferred_element_type=f32)

    return one(left[0], right[0]) + (one(left[0], right[1]) + one(left[1], right[0]))


def fold(values):
    rows, columns = values.shape
    return jnp.sum(values.reshape(rows // SUBLANES, SUBLANES, columns), axis=0)


def kernel(
    parts, groups, coef,
    plan_ref, sf_ref, tf_ref, sp_ref, tp_ref, crops_ref, crops_t_ref,
    step_ref, fgrad_ref,
    sp_in, tp_in, s_in, t_in, own_s, own_t, unit_hi, unit_lo, expo_hi, expo_lo,
    lane_part, inv_total, weighted, assign, row_dp, row_pr, tot_dp, tot_pr,
    f_send, f_pair, f_dp, f_part, f_pr, f_sum, g_send, g_dp, g_pr, moved,
    dp_send, dp_recv, pr_send, pr_recv, local_sem,
):
    me, mine = lax.axis_index("dp"), lax.axis_index("proto")
    crop_rows, width = sf_ref.shape
    teach_rows = tf_ref.shape[0]
    own_rows, columns = sp_ref.shape
    share = columns // parts
    half = parts // 2
    temp = plan_ref[1]
    parity = lax.rem(me, 2)
    partner = me + 1 - 2 * parity
    twins = [lax.rem(me + 2 * hop, parts) for hop in range(1, half)]
    senders = [lax.rem(me + parts - 2 * hop, parts) for hop in range(1, half)]
    dp_peers = [lax.rem(me + hop, parts) for hop in range(1, parts)]
    pr_peers = [lax.rem(mine + hop, groups) for hop in range(1, groups)]
    barrier = pltpu.get_barrier_semaphore()
    for peer in dp_peers:
        pl.semaphore_signal(barrier, inc=1, device_id={"dp": peer}, device_id_type=MESH)
    for peer in pr_peers:
        pl.semaphore_signal(barrier, inc=1, device_id={"proto": peer}, device_id_type=MESH)
    sends = []

    def cols(which):
        return pl.ds(pl.multiple_of(which * share, share), share)

    def rows(which, size):
        return pl.ds(pl.multiple_of(which * size, size), size)

    def dp_move(kind, hop, peer, src, dst):
        return pltpu.make_async_remote_copy(
            src_ref=src, dst_ref=dst, send_sem=dp_send.at[kind, hop], recv_sem=dp_recv.at[kind, hop],
            device_id={"dp": peer}, device_id_type=MESH,
        )

    def pr_move(kind, hop, peer, src, dst):
        return pltpu.make_async_remote_copy(
            src_ref=src, dst_ref=dst, send_sem=pr_send.at[kind, hop], recv_sem=pr_recv.at[kind, hop],
            device_id={"proto": peer}, device_id_type=MESH,
        )

    def start(moves):
        for move in moves:
            move.start()
            sends.append(move)
        return moves

    def arrive(moves):
        for move in moves:
            move.wait_recv()

    own_block = rows(me, own_rows)
    local_moves = [
        pltpu.make_async_copy(tp_ref.at[:, cols(me)], tp_in.at[own_block, :], local_sem.at[0]),
        pltpu.make_async_copy(sp_ref.at[:, cols(me)], sp_in.at[own_block, :], local_sem.at[1]),
    ]
    for move in local_moves:
        move.start()
    t_values = tf_ref[...]
    own_t[...] = t_values / jnp.sqrt(jnp.sum(t_values * t_values, axis=1, keepdims=True) + norm_eps)
    pl.semaphore_wait(barrier, parts - 1 + groups - 1)

    teacher_moves = start(
        [dp_move(0, hop, peer, tp_ref.at[:, cols(peer)], tp_in.at[own_block, :]) for hop, peer in enumerate(dp_peers)]
        + [dp_move(1, hop, peer, own_t, t_in.at[rows(me, teach_rows), :]) for hop, peer in enumerate(dp_peers)]
    )
    t_in[rows(me, teach_rows), :] = own_t[...]

    s_values = sf_ref[...]
    s_norm = jnp.sqrt(jnp.sum(s_values * s_values, axis=1, keepdims=True) + norm_eps)
    s_unit = s_values / s_norm
    teach = lax.broadcasted_iota(jnp.int32, (teach_rows, crop_rows), 0)
    same = crops_t_ref[0:1, :] == teach // GLOBAL_CROPS
    other = crops_t_ref[1:2, :] != teach % GLOBAL_CROPS
    pairs_t = jnp.where(same & other, 1.0, 0.0).astype(f32)
    mixed_at, count_at = crop_rows, crop_rows + teach_rows
    own_s[0:crop_rows, :] = s_unit
    own_s[mixed_at:count_at, :] = dot(pairs_t, s_unit, NN)
    own_s[count_at:, :] = jnp.zeros((SUBLANES, width), f32)
    own_s[count_at:, 0:crop_rows] = jnp.broadcast_to(
        jnp.sum(pairs_t, axis=0, keepdims=True), (SUBLANES, crop_rows)
    )
    near_move = start([dp_move(3, 0, partner, own_s, s_in.at[me])])
    twin_moves = start([dp_move(3, hop + 1, peer, own_s, s_in.at[me]) for hop, peer in enumerate(twins)])
    proto_moves = start(
        [dp_move(2, hop, peer, sp_ref.at[:, cols(peer)], sp_in.at[own_block, :]) for hop, peer in enumerate(dp_peers)]
    )
    s_in[me] = own_s[...]
    for move in local_moves:
        move.wait()

    def first_hop(values, first, kind):
        first[me] = values
        return start(
            [dp_move(kind, hop, peer, first.at[me], first.at[me]) for hop, peer in enumerate(dp_peers)]
        )

    def second_hop(moves, first, second, kind):
        arrive(moves)
        second[mine] = jnp.sum(first[...], axis=0)
        return start(
            [pr_move(kind, hop, peer, second.at[mine], second.at[mine]) for hop, peer in enumerate(pr_peers)]
        )

    def result(moves, second):
        arrive(moves)
        return jnp.sum(jnp.sum(second[...], axis=0), axis=0, keepdims=True)

    def balance(scale):
        values = assign[...]
        if scale is not None:
            values = values * scale
        values = values * (1.0 / jnp.sum(values, axis=1, keepdims=True))
        assign[...] = values
        return fold(values)

    def f_move(step, block):
        return dp_move(9, step, partner, f_send.at[block], f_pair.at[block // 2])

    def crop_blocks(base, near):
        def crop_block(step, carry):
            block = lax.rem(base + 2 * step, parts)
            at = rows(block, crop_rows)
            unit = (unit_hi[...], unit_lo[...])
            expo = jnp.exp(dot3(split(s_in[block, 0:crop_rows, :]), unit, NN) / student_temp)
            part = expo[:, 0:LANES]
            for lane in range(1, share // LANES):
                part = part + expo[:, lane * LANES:(lane + 1) * LANES]
            lane_part[at, :] = part
            pieces = split(expo)
            expo_hi[at, :] = pieces[0]
            expo_lo[at, :] = pieces[1]
            f_send[block] = dot3(pieces, unit, NT)
            if near:
                f_move(step, block).start()
            return carry

        lax.fori_loop(0, half, crop_block, 0)

    arrive(teacher_moves)
    teacher_cols = tp_in[...]
    teacher_norm = jnp.sqrt(jnp.sum(teacher_cols * teacher_cols, axis=0, keepdims=True) + norm_eps)
    assign[...] = jnp.exp(dot((teacher_cols / teacher_norm).T, t_in[...], NT) / temp)
    near = first_hop(balance(None), row_dp.at[0], 4)
    near = second_hop(near, row_dp.at[0], row_pr.at[0], 0)
    arrive(twin_moves)
    onward = start(
        [dp_move(8, hop, partner, s_in.at[block], s_in.at[block]) for hop, block in enumerate(senders)]
    )
    scale = 1.0 / result(near, row_pr.at[0])
    near = first_hop(balance(scale), row_dp.at[1], 5)

    arrive(proto_moves)
    student_cols = sp_in[...]
    student_norm = jnp.sqrt(jnp.sum(student_cols * student_cols, axis=0, keepdims=True) + norm_eps)
    high, low = split(student_cols / student_norm)
    unit_hi[...] = high
    unit_lo[...] = low
    arrive(near_move + onward)
    crop_blocks(partner, True)
    near = second_hop(near, row_dp.at[1], row_pr.at[1], 1)
    crop_blocks(me, False)
    tot_near = first_hop(fold(lane_part[...].T), tot_dp, 7)
    scale = 1.0 / result(near, row_pr.at[1])
    near = first_hop(balance(scale), row_dp.at[2], 6)

    f_near = [f_move(step, lax.rem(partner + 2 * step, parts)) for step in range(half)]
    arrive(f_near)
    sends.extend(f_near)
    slot = me // 2
    f_moves = []
    for hop, peer in enumerate(twins):
        f_send[peer] = f_send[peer] + f_pair[peer // 2]
        f_moves.append(dp_move(10, hop, peer, f_send.at[peer], f_dp.at[slot]))
        start(f_moves[-1:])
    f_dp[slot] = f_send[me] + f_pair[slot]
    tot_near = second_hop(tot_near, tot_dp, tot_pr, 3)
    near = second_hop(near, row_dp.at[2], row_pr.at[2], 2)
    mixed = s_in[:, mixed_at:count_at, :].reshape(parts * teach_rows, width).T
    targets = dot3((unit_hi[...], unit_lo[...]), split(assign[...]), NN)
    total = result(tot_near, tot_pr)
    inv_total[...] = jnp.broadcast_to(1.0 / total, (LANES, parts * crop_rows)).T
    for block in range(parts):
        at = slice(block * crop_rows, (block + 1) * crop_rows)
        count = jnp.broadcast_to(s_in[block, count_at:count_at + 1, :], (LANES, width)).T
        weight = count[0:crop_rows, :] * inv_total[at, :]
        weighted[at, :] = s_in[block, 0:crop_rows, :] * jnp.concatenate([weight] * (width // LANES), axis=1)
    weighted_t = split(weighted[...].T)
    scale = 1.0 / result(near, row_pr.at[2])
    mixed_t = split(mixed * scale)
    g_send[...] = (targets * scale).T

    chunk = share // 2
    back_moves = []
    for piece in range(2):
        at = slice(piece * chunk, (piece + 1) * chunk)
        grad = coef * (
            dot3(weighted_t, (expo_hi[:, at], expo_lo[:, at]), NN)
            - dot3(mixed_t, split(assign[at, :]), NT)
        )
        now = sp_in[:, at]
        norm = jnp.sqrt(jnp.sum(now * now, axis=0, keepdims=True) + norm_eps)
        unit = now / norm
        proto_grad = (grad - unit * jnp.sum(unit * grad, axis=0, keepdims=True)) / norm
        square = jnp.sum(proto_grad * proto_grad, axis=0, keepdims=True) / width
        moved[:, at] = proto_grad / jnp.sqrt(square + square_eps)
        place = pl.ds(pl.multiple_of(me * share + piece * chunk, chunk), chunk)
        back_moves += start([
            dp_move(12 + piece, hop, peer, moved.at[rows(peer, own_rows), at], step_ref.at[:, place])
            for hop, peer in enumerate(dp_peers)
        ])
        step_ref[:, place] = moved[own_block, at]
        if piece == 0:
            g_moves = start([
                dp_move(11, hop, peer, g_send.at[rows(peer, teach_rows), :], g_dp.at[me])
                for hop, peer in enumerate(dp_peers)
            ])
            g_dp[me] = g_send[rows(me, teach_rows), :]

    piece_rows = f_part.shape[0] // groups
    arrive(f_moves)
    f_part[0:crop_rows, :] = jnp.sum(f_dp[...], axis=0)
    if f_part.shape[0] > crop_rows:
        f_part[crop_rows:, :] = jnp.zeros((f_part.shape[0] - crop_rows, width), f32)
    f_across = start(
        [pr_move(4, hop, peer, f_part.at[rows(peer, piece_rows), :], f_pr.at[mine]) for hop, peer in enumerate(pr_peers)]
    )
    f_pr[mine] = f_part[rows(mine, piece_rows), :]
    arrive(g_moves)
    g_pr[mine] = jnp.sum(g_dp[...], axis=0)
    g_across = start(
        [pr_move(5, hop, peer, g_pr.at[mine], g_pr.at[mine]) for hop, peer in enumerate(pr_peers)]
    )
    arrive(f_across)
    own_piece = rows(mine, piece_rows)
    f_sum[own_piece, :] = jnp.sum(f_pr[...], axis=0)
    f_last = start(
        [pr_move(6, hop, peer, f_sum.at[own_piece, :], f_sum.at[own_piece, :]) for hop, peer in enumerate(pr_peers)]
    )
    teach = lax.broadcasted_iota(jnp.int32, (crop_rows, teach_rows), 1)
    same = crops_ref[:, 0:1] == teach // GLOBAL_CROPS
    other = crops_ref[:, 1:2] != teach % GLOBAL_CROPS
    pairs = jnp.where(same & other, 1.0, 0.0).astype(f32)
    count = jnp.sum(pairs, axis=1, keepdims=True)
    inverse = jnp.concatenate([inv_total[rows(me, crop_rows), :]] * (width // LANES), axis=1)
    s_values = sf_ref[...]
    s_norm = jnp.sqrt(jnp.sum(s_values * s_values, axis=1, keepdims=True) + norm_eps)
    s_unit = s_values / s_norm
    arrive(g_across)
    wanted = dot(pairs, jnp.sum(g_pr[...], axis=0), NN)
    arrive(f_last)
    feature_unit = coef * (count * (f_sum[0:crop_rows, :] * inverse) - wanted)
    fgrad_ref[...] = (
        feature_unit - s_unit * jnp.sum(s_unit * feature_unit, axis=1, keepdims=True)
    ) / s_norm
    arrive(back_moves)
    for move in sends:
        move.wait_send()


def body(student_feats, teacher_feats, student_proto, teacher_proto, crops, step):
    parts, groups = lax.axis_size("dp"), lax.axis_size("proto")
    crop_rows, width = student_feats.shape
    teach_rows = teacher_feats.shape[0]
    own_rows, columns = student_proto.shape
    share = columns // parts
    images = teach_rows // GLOBAL_CROPS * parts
    pair_total = GLOBAL_CROPS * (GLOBAL_CROPS - 1) + (CROPS - GLOBAL_CROPS) * GLOBAL_CROPS
    coef = loss_scale / (pair_total * images * student_temp)
    all_s, all_t = parts * crop_rows, parts * teach_rows
    packed = crop_rows + teach_rows + SUBLANES
    kinds = 14
    piece_rows = -(-crop_rows // (groups * SUBLANES)) * SUBLANES
    rate, teacher_temp, momentum = plan(step)

    def vmem(*shape, dtype=f32):
        return pltpu.VMEM(shape, dtype)

    def sems(*shape):
        return pltpu.SemaphoreType.DMA(shape)

    whole = pl.BlockSpec(memory_space=pltpu.VMEM)
    shapes = [student_proto, student_feats]
    direction, feature_grad = pl.pallas_call(
        functools.partial(kernel, parts, groups, coef),
        out_shape=[jax.ShapeDtypeStruct(one.shape, f32) for one in shapes],
        in_specs=[pl.BlockSpec(memory_space=pltpu.SMEM)] + [whole] * 6,
        out_specs=[whole] * 2,
        scratch_shapes=[
            vmem(width, share), vmem(width, share),
            vmem(parts, packed, width), vmem(all_t, width),
            vmem(packed, width), vmem(teach_rows, width),
            vmem(width, share, dtype=bf16), vmem(width, share, dtype=bf16),
            vmem(all_s, share, dtype=bf16), vmem(all_s, share, dtype=bf16),
            vmem(all_s, LANES), vmem(all_s, LANES), vmem(all_s, width),
            vmem(share, all_t),
            vmem(ITERS, parts, SUBLANES, all_t), vmem(ITERS, groups, SUBLANES, all_t),
            vmem(parts, SUBLANES, all_s), vmem(groups, SUBLANES, all_s),
            vmem(parts, crop_rows, width), vmem(parts // 2, crop_rows, width),
            vmem(parts // 2, crop_rows, width), vmem(groups * piece_rows, width),
            vmem(groups, piece_rows, width), vmem(groups * piece_rows, width),
            vmem(all_t, width), vmem(parts, teach_rows, width), vmem(groups, teach_rows, width),
            vmem(width, share),
            sems(kinds, parts), sems(kinds, parts), sems(7, groups), sems(7, groups), sems(2),
        ],
        compiler_params=pltpu.CompilerParams(
            collective_id=0, has_side_effects=True, vmem_limit_bytes=56 * 1024 * 1024
        ),
    )(jnp.stack([rate, teacher_temp]), student_feats, teacher_feats, student_proto, teacher_proto, crops, crops.T)
    student_next = student_proto - rate * (direction + weight_decay * student_proto)
    teacher_next = momentum * teacher_proto + (1.0 - momentum) * student_next
    return (student_next, teacher_next, feature_grad)


def solution(mesh):
    in_specs = (
        P("dp", None),
        P("dp", None),
        P("dp", "proto"),
        P("dp", "proto"),
        P("dp", None),
        P(),
    )
    out_specs = (P("dp", "proto"), P("dp", "proto"), P("dp", None))
    return jax.shard_map(body, mesh=mesh, in_specs=in_specs, out_specs=out_specs, check_vma=False)
```

time: 133 us -> 99 us (0.74)
  the two profiles are of different devices: /device:TPU:26 before, /device:TPU:0 now
where the time goes in v3:
time: 99 us; the launch traced here: 98 us
  Pallas kernels  91.7 us (93%)
  other arithmetic  3.41 us (3%)
  local copies, waits for them, and re-layouts  1.52 us (2%)
  between operations  1.41 us (1%)
    pallas_call x1, Pallas kernels, body(): pl.pallas_call(functools.partial(kernel, parts, groups, coef), out_shape=...  91.7 us
    add x1, other arithmetic, body(): teacher_next = momentum * teacher_proto + (1.0 - momentum) * student_next  2.82 us

profile of v3, /device:TPU:0, one launch (start us, length us, event | category | flops | bytes accessed | tf_op | source)
XLA Modules:
  0.0 98.0 jit_solution(14637734872539868626)
XLA Ops:
  1.4 0.0 copy-start.3
  1.4 0.6 pad_maximum_fusion.plan_ref
  2.0 0.1 copy-done.3
  2.1 0.8 copy.9.crops_ref
  2.8 0.0 copy-start
  2.8 0.0 copy-start.1
  2.8 91.7 %shard_map.85 = (f32[32,8192]{1,0:T(8,128)}, f32[160,256]{1,0:T(8,128)}) custom-call(f32[2]{0:T(128)} %pad_maximum_fusion.plan_ref, f32[160,256]{1,0:T(8,128)} %sf_ref.1, f32[32,256]{1,0:T(8,128)} %tf_ref.1, f32[32,8192]{1,0:T(8,128)} %sp_ref.1, f32[32,8192]{1,0:T(8,128)} %tp_ref.1, s32[160,2]{1,0:T(8,128)} %copy.9.crops_ref, s32[2,160]{1,0:T(2,128)} %bitcast.3), custom_call_target="tpu_custom_call" | custom-call | tf_op jit(solution)/shard_map/pallas_call | solution.py:355
  94.5 0.0 copy-done
  94.5 0.0 copy-done.1
  94.5 0.0 copy-start.2
  94.5 2.8 %multiply_add_fusion = (f32[32,8192]{1,0:T(8,128)}, f32[32,8192]{1,0:T(8,128)}) fusion(f32[32,8192]{1,0:T(8,128)S(1)} %copy-done, f32[]{:T(128)S(6)} %sub.11, f32[]{:T(128)} %bitcast.2, f32[32,8192]{1,0:T(8,128)S(1)} %copy-done.1, f32[32,8192]{1,0:T(8,128)} %get-tuple-element.5, f32[]{:T(128)} %bitcast), kind=kLoop, calls=%fused_computation | loop fusion | flops 1835008 | bytes 5242892 | tf_op jit(solution)/shard_map/add | solution.py:382
  97.3 0.0 copy-done.2
  97.3 0.7 copy.12
Async XLA Ops:
  1.4 0.7 copy-start.3
  2.8 91.7 %copy-start = (f32[32,8192]{1,0:T(8,128)S(1)}, f32[32,8192]{1,0:T(8,128)}, u32[]{:S(2)}) copy-start(f32[32,8192]{1,0:T(8,128)} %tp_ref.1) | copy-start | bytes 3145732
  2.8 91.7 %copy-start.1 = (f32[32,8192]{1,0:T(8,128)S(1)}, f32[32,8192]{1,0:T(8,128)}, u32[]{:S(2)}) copy-start(f32[32,8192]{1,0:T(8,128)} %sp_ref.1) | copy-start | bytes 3145732
  94.5 2.8 %copy-start.2 = (f32[160,256]{1,0:T(8,128)S(1)}, f32[160,256]{1,0:T(8,128)}, u32[]{:S(2)}) copy-start(f32[160,256]{1,0:T(8,128)} %get-tuple-element.14) | copy-start | bytes 491524

commit v4 on v3

--- a/solution.py
+++ b/solution.py
@@ -38,6 +38,7 @@
 MESH = pl.DeviceIdType.MESH
 LANES = 128
 SUBLANES = 8
+CHUNKS = 4
 f32 = jnp.float32
 bf16 = jnp.bfloat16
 
@@ -68,7 +69,7 @@
     plan_ref, sf_ref, tf_ref, sp_ref, tp_ref, crops_ref, crops_t_ref,
     step_ref, fgrad_ref,
     sp_in, tp_in, s_in, t_in, own_s, own_t, unit_hi, unit_lo, expo_hi, expo_lo,
-    lane_part, inv_total, weighted, assign, row_dp, row_pr, tot_dp, tot_pr,
+    s_hi, s_lo, lane_part, counted, counted_t, mixed_t, assign, row_dp, row_pr, tot_dp, tot_pr,
     f_send, f_pair, f_dp, f_part, f_pr, f_sum, g_send, g_dp, g_pr, moved,
     dp_send, dp_recv, pr_send, pr_recv, local_sem,
 ):
@@ -185,28 +186,38 @@
         assign[...] = values
         return fold(values)
 
-    def f_move(step, block):
-        return dp_move(9, step, partner, f_send.at[block], f_pair.at[block // 2])
-
-    def crop_blocks(base, near):
-        def crop_block(step, carry):
-            block = lax.rem(base + 2 * step, parts)
-            at = rows(block, crop_rows)
-            unit = (unit_hi[...], unit_lo[...])
-            expo = jnp.exp(dot3(split(s_in[block, 0:crop_rows, :]), unit, NN) / student_temp)
-            part = expo[:, 0:LANES]
-            for lane in range(1, share // LANES):
-                part = part + expo[:, lane * LANES:(lane + 1) * LANES]
-            lane_part[at, :] = part
-            pieces = split(expo)
-            expo_hi[at, :] = pieces[0]
-            expo_lo[at, :] = pieces[1]
-            f_send[block] = dot3(pieces, unit, NT)
+    tile = 2 * crop_rows
+    half_rows = half * crop_rows
+
+    def place_of(block):
+        return (block // 2) + half * lax.rem(block, 2)
+
+    def score_tile(step, carry):
+        at = rows(step, tile)
+        unit = (unit_hi[...], unit_lo[...])
+        expo = jnp.exp(dot3((s_hi[at, :], s_lo[at, :]), unit, NN) / student_temp)
+        part = expo[:, 0:LANES]
+        for lane in range(1, share // LANES):
+            part = part + expo[:, lane * LANES:(lane + 1) * LANES]
+        lane_part[at, :] = part
+        pieces = split(expo)
+        expo_hi[at, :] = pieces[0]
+        expo_lo[at, :] = pieces[1]
+        return carry
+
+    def f_move(step):
+        at = pl.ds(pl.multiple_of((1 - parity) * half_rows + step * tile, tile), tile)
+        return dp_move(9, step, partner, f_send.at[at, :], f_pair.at[rows(step, tile), :])
+
+    def feature_tiles(which, near):
+        def feature_tile(step, carry):
+            at = pl.ds(pl.multiple_of(which * half_rows + step * tile, tile), tile)
+            f_send[at, :] = dot3((expo_hi[at, :], expo_lo[at, :]), (unit_hi[...], unit_lo[...]), NT)
             if near:
-                f_move(step, block).start()
+                f_move(step).start()
             return carry
 
-        lax.fori_loop(0, half, crop_block, 0)
+        lax.fori_loop(0, half // 2, feature_tile, 0)
 
     arrive(teacher_moves)
     teacher_cols = tp_in[...]
@@ -214,12 +225,28 @@
     assign[...] = jnp.exp(dot((teacher_cols / teacher_norm).T, t_in[...], NT) / temp)
     near = first_hop(balance(None), row_dp.at[0], 4)
     near = second_hop(near, row_dp.at[0], row_pr.at[0], 0)
+    scale = 1.0 / result(near, row_pr.at[0])
+    near = first_hop(balance(scale), row_dp.at[1], 5)
     arrive(twin_moves)
     onward = start(
         [dp_move(8, hop, partner, s_in.at[block], s_in.at[block]) for hop, block in enumerate(senders)]
     )
-    scale = 1.0 / result(near, row_pr.at[0])
-    near = first_hop(balance(scale), row_dp.at[1], 5)
+    near = second_hop(near, row_dp.at[1], row_pr.at[1], 1)
+    scale = 1.0 / result(near, row_pr.at[1])
+    near = first_hop(balance(scale), row_dp.at[2], 6)
+
+    arrive(near_move + onward)
+    for block in range(parts):
+        first = (block // 2 + half * (block % 2)) * crop_rows
+        at = slice(first, first + crop_rows)
+        crops_now = s_in[block, 0:crop_rows, :]
+        high, low = split(crops_now)
+        s_hi[at, :] = high
+        s_lo[at, :] = low
+        count = jnp.broadcast_to(s_in[block, count_at:count_at + 1, :], (LANES, width)).T
+        counted[at, :] = crops_now * jnp.concatenate([count[0:crop_rows, :]] * (width // LANES), axis=1)
+    counted_t[...] = counted[...].T
+    mixed_t[...] = s_in[:, mixed_at:count_at, :].reshape(parts * teach_rows, width).T
 
     arrive(proto_moves)
     student_cols = sp_in[...]
@@ -227,47 +254,39 @@
     high, low = split(student_cols / student_norm)
     unit_hi[...] = high
     unit_lo[...] = low
-    arrive(near_move + onward)
-    crop_blocks(partner, True)
-    near = second_hop(near, row_dp.at[1], row_pr.at[1], 1)
-    crop_blocks(me, False)
+    near = second_hop(near, row_dp.at[2], row_pr.at[2], 2)
+    lax.fori_loop(0, half, score_tile, 0)
     tot_near = first_hop(fold(lane_part[...].T), tot_dp, 7)
-    scale = 1.0 / result(near, row_pr.at[1])
-    near = first_hop(balance(scale), row_dp.at[2], 6)
-
-    f_near = [f_move(step, lax.rem(partner + 2 * step, parts)) for step in range(half)]
+    feature_tiles(1 - parity, True)
+    tot_near = second_hop(tot_near, tot_dp, tot_pr, 3)
+    feature_tiles(parity, False)
+    targets = dot3((unit_hi[...], unit_lo[...]), split(assign[...]), NN)
+    scale = 1.0 / result(near, row_pr.at[2])
+    mixed_pieces = split(mixed_t[...] * scale)
+    g_send[...] = (targets * scale).T
+    f_near = [f_move(step) for step in range(half // 2)]
     arrive(f_near)
     sends.extend(f_near)
+    own_half = pl.ds(pl.multiple_of(parity * half_rows, half_rows), half_rows)
+    f_send[own_half, :] = f_send[own_half, :] + f_pair[...]
     slot = me // 2
-    f_moves = []
-    for hop, peer in enumerate(twins):
-        f_send[peer] = f_send[peer] + f_pair[peer // 2]
-        f_moves.append(dp_move(10, hop, peer, f_send.at[peer], f_dp.at[slot]))
-        start(f_moves[-1:])
-    f_dp[slot] = f_send[me] + f_pair[slot]
-    tot_near = second_hop(tot_near, tot_dp, tot_pr, 3)
-    near = second_hop(near, row_dp.at[2], row_pr.at[2], 2)
-    mixed = s_in[:, mixed_at:count_at, :].reshape(parts * teach_rows, width).T
-    targets = dot3((unit_hi[...], unit_lo[...]), split(assign[...]), NN)
-    total = result(tot_near, tot_pr)
-    inv_total[...] = jnp.broadcast_to(1.0 / total, (LANES, parts * crop_rows)).T
-    for block in range(parts):
-        at = slice(block * crop_rows, (block + 1) * crop_rows)
-        count = jnp.broadcast_to(s_in[block, count_at:count_at + 1, :], (LANES, width)).T
-        weight = count[0:crop_rows, :] * inv_total[at, :]
-        weighted[at, :] = s_in[block, 0:crop_rows, :] * jnp.concatenate([weight] * (width // LANES), axis=1)
-    weighted_t = split(weighted[...].T)
-    scale = 1.0 / result(near, row_pr.at[2])
-    mixed_t = split(mixed * scale)
-    g_send[...] = (targets * scale).T
-
-    chunk = share // 2
-    back_moves = []
-    for piece in range(2):
+    f_moves = start([
+        dp_move(10, hop, peer, f_send.at[rows(place_of(peer), crop_rows), :], f_dp.at[slot])
+        for hop, peer in enumerate(twins)
+    ])
+    f_dp[slot] = f_send[rows(place_of(me), crop_rows), :]
+    inverse_row = 1.0 / result(tot_near, tot_pr)
+    weighted_t = split(counted_t[...] * inverse_row)
+    lane_part[...] = jnp.broadcast_to(inverse_row, (LANES, parts * crop_rows)).T
+
+    chunk = share // CHUNKS
+    piece_rows = f_part.shape[0] // groups
+    back_moves, home_moves = [], []
+    for piece in range(CHUNKS):
         at = slice(piece * chunk, (piece + 1) * chunk)
         grad = coef * (
             dot3(weighted_t, (expo_hi[:, at], expo_lo[:, at]), NN)
-            - dot3(mixed_t, split(assign[at, :]), NT)
+            - dot3(mixed_pieces, split(assign[at, :]), NT)
         )
         now = sp_in[:, at]
         norm = jnp.sqrt(jnp.sum(now * now, axis=0, keepdims=True) + norm_eps)
@@ -280,40 +299,41 @@
             dp_move(12 + piece, hop, peer, moved.at[rows(peer, own_rows), at], step_ref.at[:, place])
             for hop, peer in enumerate(dp_peers)
         ])
-        step_ref[:, place] = moved[own_block, at]
+        home_moves.append(pltpu.make_async_copy(moved.at[own_block, at], step_ref.at[:, place], local_sem.at[2 + piece]))
+        home_moves[-1].start()
         if piece == 0:
             g_moves = start([
                 dp_move(11, hop, peer, g_send.at[rows(peer, teach_rows), :], g_dp.at[me])
                 for hop, peer in enumerate(dp_peers)
             ])
             g_dp[me] = g_send[rows(me, teach_rows), :]
-
-    piece_rows = f_part.shape[0] // groups
-    arrive(f_moves)
-    f_part[0:crop_rows, :] = jnp.sum(f_dp[...], axis=0)
-    if f_part.shape[0] > crop_rows:
-        f_part[crop_rows:, :] = jnp.zeros((f_part.shape[0] - crop_rows, width), f32)
-    f_across = start(
-        [pr_move(4, hop, peer, f_part.at[rows(peer, piece_rows), :], f_pr.at[mine]) for hop, peer in enumerate(pr_peers)]
-    )
-    f_pr[mine] = f_part[rows(mine, piece_rows), :]
-    arrive(g_moves)
-    g_pr[mine] = jnp.sum(g_dp[...], axis=0)
-    g_across = start(
-        [pr_move(5, hop, peer, g_pr.at[mine], g_pr.at[mine]) for hop, peer in enumerate(pr_peers)]
-    )
+        if piece == 1:
+            arrive(f_moves)
+            f_part[0:crop_rows, :] = jnp.sum(f_dp[...], axis=0)
+            if f_part.shape[0] > crop_rows:
+                f_part[crop_rows:, :] = jnp.zeros((f_part.shape[0] - crop_rows, width), f32)
+            f_across = start([
+                pr_move(4, hop, peer, f_part.at[rows(peer, piece_rows), :], f_pr.at[mine])
+                for hop, peer in enumerate(pr_peers)
+            ])
+            f_pr[mine] = f_part[rows(mine, piece_rows), :]
     arrive(f_across)
     own_piece = rows(mine, piece_rows)
     f_sum[own_piece, :] = jnp.sum(f_pr[...], axis=0)
     f_last = start(
         [pr_move(6, hop, peer, f_sum.at[own_piece, :], f_sum.at[own_piece, :]) for hop, peer in enumerate(pr_peers)]
     )
+    arrive(g_moves)
+    g_pr[mine] = jnp.sum(g_dp[...], axis=0)
+    g_across = start(
+        [pr_move(5, hop, peer, g_pr.at[mine], g_pr.at[mine]) for hop, peer in enumerate(pr_peers)]
+    )
     teach = lax.broadcasted_iota(jnp.int32, (crop_rows, teach_rows), 1)
     same = crops_ref[:, 0:1] == teach // GLOBAL_CROPS
     other = crops_ref[:, 1:2] != teach % GLOBAL_CROPS
     pairs = jnp.where(same & other, 1.0, 0.0).astype(f32)
     count = jnp.sum(pairs, axis=1, keepdims=True)
-    inverse = jnp.concatenate([inv_total[rows(me, crop_rows), :]] * (width // LANES), axis=1)
+    inverse = jnp.concatenate([lane_part[rows(place_of(me), crop_rows), :]] * (width // LANES), axis=1)
     s_values = sf_ref[...]
     s_norm = jnp.sqrt(jnp.sum(s_values * s_values, axis=1, keepdims=True) + norm_eps)
     s_unit = s_values / s_norm
@@ -325,6 +345,8 @@
         feature_unit - s_unit * jnp.sum(s_unit * feature_unit, axis=1, keepdims=True)
     ) / s_norm
     arrive(back_moves)
+    for move in home_moves:
+        move.wait()
     for move in sends:
         move.wait_send()
 
@@ -340,7 +362,7 @@
     coef = loss_scale / (pair_total * images * student_temp)
     all_s, all_t = parts * crop_rows, parts * teach_rows
     packed = crop_rows + teach_rows + SUBLANES
-    kinds = 14
+    kinds = 12 + CHUNKS
     piece_rows = -(-crop_rows // (groups * SUBLANES)) * SUBLANES
     rate, teacher_temp, momentum = plan(step)
 
@@ -350,29 +372,30 @@
     def sems(*shape):
         return pltpu.SemaphoreType.DMA(shape)
 
-    whole = pl.BlockSpec(memory_space=pltpu.VMEM)
+    whole, outside = pl.BlockSpec(memory_space=pltpu.VMEM), pl.BlockSpec(memory_space=pl.ANY)
     shapes = [student_proto, student_feats]
     direction, feature_grad = pl.pallas_call(
         functools.partial(kernel, parts, groups, coef),
         out_shape=[jax.ShapeDtypeStruct(one.shape, f32) for one in shapes],
-        in_specs=[pl.BlockSpec(memory_space=pltpu.SMEM)] + [whole] * 6,
-        out_specs=[whole] * 2,
+        in_specs=[pl.BlockSpec(memory_space=pltpu.SMEM), whole, whole, outside, outside, whole, whole],
+        out_specs=[outside, whole],
         scratch_shapes=[
             vmem(width, share), vmem(width, share),
             vmem(parts, packed, width), vmem(all_t, width),
             vmem(packed, width), vmem(teach_rows, width),
             vmem(width, share, dtype=bf16), vmem(width, share, dtype=bf16),
             vmem(all_s, share, dtype=bf16), vmem(all_s, share, dtype=bf16),
-            vmem(all_s, LANES), vmem(all_s, LANES), vmem(all_s, width),
+            vmem(all_s, width, dtype=bf16), vmem(all_s, width, dtype=bf16),
+            vmem(all_s, LANES), vmem(all_s, width), vmem(width, all_s), vmem(width, all_t),
             vmem(share, all_t),
             vmem(ITERS, parts, SUBLANES, all_t), vmem(ITERS, groups, SUBLANES, all_t),
             vmem(parts, SUBLANES, all_s), vmem(groups, SUBLANES, all_s),
-            vmem(parts, crop_rows, width), vmem(parts // 2, crop_rows, width),
+            vmem(all_s, width), vmem(all_s // 2, width),
             vmem(parts // 2, crop_rows, width), vmem(groups * piece_rows, width),
             vmem(groups, piece_rows, width), vmem(groups * piece_rows, width),
             vmem(all_t, width), vmem(parts, teach_rows, width), vmem(groups, teach_rows, width),
             vmem(width, share),
-            sems(kinds, parts), sems(kinds, parts), sems(7, groups), sems(7, groups), sems(2),
+            sems(kinds, parts), sems(kinds, parts), sems(7, groups), sems(7, groups), sems(2 + CHUNKS),
         ],
         compiler_params=pltpu.CompilerParams(
             collective_id=0, has_side_effects=True, vmem_limit_bytes=56 * 1024 * 1024

time: 99 us -> 103 us (1.040)
  Pallas kernels: 91.7 us -> 96 us
    pallas_call x1, Pallas kernels: 91.7 us -> 96 us  [body(): pl.pallas_call(functools.partial(kernel, parts, groups, coef), out_shape=...]
where the time goes in v4:
time: 103 us; the launch traced here: 102 us
  Pallas kernels  96 us (93%)
  other arithmetic  3.41 us (3%)
  local copies, waits for them, and re-layouts  1.52 us (1%)
  between operations  1.41 us (1%)
    pallas_call x1, Pallas kernels, body(): pl.pallas_call(functools.partial(kernel, parts, groups, coef), out_shape=...  96 us
    add x1, other arithmetic, body(): teacher_next = momentum * teacher_proto + (1.0 - momentum) * student_next  2.82 us

profile of v4, /device:TPU:0, one launch (start us, length us, event | category | flops | bytes accessed | tf_op | source)
XLA Modules:
  0.0 102.3 jit_solution(14998702788262510401)
XLA Ops:
  1.4 0.0 copy-start.3
  1.4 0.6 pad_maximum_fusion.plan_ref
  2.0 0.1 copy-done.3
  2.1 0.8 copy.9.crops_ref
  2.8 0.0 copy-start
  2.8 0.0 copy-start.1
  2.8 96.0 %shard_map.85 = (f32[32,8192]{1,0:T(8,128)}, f32[160,256]{1,0:T(8,128)}) custom-call(f32[2]{0:T(128)} %pad_maximum_fusion.plan_ref, f32[160,256]{1,0:T(8,128)} %sf_ref.1, f32[32,256]{1,0:T(8,128)} %tf_ref.1, f32[32,8192]{1,0:T(8,128)} %sp_ref.1, f32[32,8192]{1,0:T(8,128)} %tp_ref.1, s32[160,2]{1,0:T(8,128)} %copy.9.crops_ref, s32[2,160]{1,0:T(2,128)} %bitcast.3), custom_call_target="tpu_custom_call" | custom-call | tf_op jit(solution)/shard_map/pallas_call | solution.py:377
  98.8 0.0 copy-done
  98.8 0.0 copy-done.1
  98.8 0.0 copy-start.2
  98.9 2.8 %multiply_add_fusion = (f32[32,8192]{1,0:T(8,128)}, f32[32,8192]{1,0:T(8,128)}) fusion(f32[32,8192]{1,0:T(8,128)S(1)} %copy-done, f32[]{:T(128)S(6)} %sub.11, f32[]{:T(128)} %bitcast.2, f32[32,8192]{1,0:T(8,128)S(1)} %copy-done.1, f32[32,8192]{1,0:T(8,128)} %get-tuple-element.5, f32[]{:T(128)} %bitcast), kind=kLoop, calls=%fused_computation | loop fusion | flops 1835008 | bytes 5242892 | tf_op jit(solution)/shard_map/add | solution.py:405
  101.7 0.0 copy-done.2
  101.7 0.7 copy.12
Async XLA Ops:
  1.4 0.7 copy-start.3
  2.8 96.0 %copy-start = (f32[32,8192]{1,0:T(8,128)S(1)}, f32[32,8192]{1,0:T(8,128)}, u32[]{:S(2)}) copy-start(f32[32,8192]{1,0:T(8,128)} %tp_ref.1) | copy-start | bytes 3145732
  2.8 96.0 %copy-start.1 = (f32[32,8192]{1,0:T(8,128)S(1)}, f32[32,8192]{1,0:T(8,128)}, u32[]{:S(2)}) copy-start(f32[32,8192]{1,0:T(8,128)} %sp_ref.1) | copy-start | bytes 3145732
  98.8 2.8 %copy-start.2 = (f32[160,256]{1,0:T(8,128)S(1)}, f32[160,256]{1,0:T(8,128)}, u32[]{:S(2)}) copy-start(f32[160,256]{1,0:T(8,128)} %get-tuple-element.14) | copy-start | bytes 491524

commit v5 on v4

--- a/solution.py
+++ b/solution.py
@@ -152,11 +152,6 @@
     own_s[count_at:, 0:crop_rows] = jnp.broadcast_to(
         jnp.sum(pairs_t, axis=0, keepdims=True), (SUBLANES, crop_rows)
     )
-    near_move = start([dp_move(3, 0, partner, own_s, s_in.at[me])])
-    twin_moves = start([dp_move(3, hop + 1, peer, own_s, s_in.at[me]) for hop, peer in enumerate(twins)])
-    proto_moves = start(
-        [dp_move(2, hop, peer, sp_ref.at[:, cols(peer)], sp_in.at[own_block, :]) for hop, peer in enumerate(dp_peers)]
-    )
     s_in[me] = own_s[...]
     for move in local_moves:
         move.wait()
@@ -224,17 +219,19 @@
     teacher_norm = jnp.sqrt(jnp.sum(teacher_cols * teacher_cols, axis=0, keepdims=True) + norm_eps)
     assign[...] = jnp.exp(dot((teacher_cols / teacher_norm).T, t_in[...], NT) / temp)
     near = first_hop(balance(None), row_dp.at[0], 4)
+    near_move = start([dp_move(3, 0, partner, own_s, s_in.at[me])])
+    twin_moves = start([dp_move(3, hop + 1, peer, own_s, s_in.at[me]) for hop, peer in enumerate(twins)])
     near = second_hop(near, row_dp.at[0], row_pr.at[0], 0)
     scale = 1.0 / result(near, row_pr.at[0])
     near = first_hop(balance(scale), row_dp.at[1], 5)
+    proto_moves = start(
+        [dp_move(2, hop, peer, sp_ref.at[:, cols(peer)], sp_in.at[own_block, :]) for hop, peer in enumerate(dp_peers)]
+    )
     arrive(twin_moves)
     onward = start(
         [dp_move(8, hop, partner, s_in.at[block], s_in.at[block]) for hop, block in enumerate(senders)]
     )
     near = second_hop(near, row_dp.at[1], row_pr.at[1], 1)
-    scale = 1.0 / result(near, row_pr.at[1])
-    near = first_hop(balance(scale), row_dp.at[2], 6)
-
     arrive(near_move + onward)
     for block in range(parts):
         first = (block // 2 + half * (block % 2)) * crop_rows
@@ -248,15 +245,18 @@
     counted_t[...] = counted[...].T
     mixed_t[...] = s_in[:, mixed_at:count_at, :].reshape(parts * teach_rows, width).T
 
+    scale = 1.0 / result(near, row_pr.at[1])
+    near = first_hop(balance(scale), row_dp.at[2], 6)
+
     arrive(proto_moves)
     student_cols = sp_in[...]
     student_norm = jnp.sqrt(jnp.sum(student_cols * student_cols, axis=0, keepdims=True) + norm_eps)
     high, low = split(student_cols / student_norm)
     unit_hi[...] = high
     unit_lo[...] = low
-    near = second_hop(near, row_dp.at[2], row_pr.at[2], 2)
     lax.fori_loop(0, half, score_tile, 0)
     tot_near = first_hop(fold(lane_part[...].T), tot_dp, 7)
+    near = second_hop(near, row_dp.at[2], row_pr.at[2], 2)
     feature_tiles(1 - parity, True)
     tot_near = second_hop(tot_near, tot_dp, tot_pr, 3)
     feature_tiles(parity, False)

time: 103 us -> 90.6 us (0.88)
  Pallas kernels: 96 us -> 84.1 us
    pallas_call x1, Pallas kernels: 96 us -> 84.1 us  [body(): pl.pallas_call(functools.partial(kernel, parts, groups, coef), out_shape=...]
where the time goes in v5:
time: 90.6 us; the launch traced here: 90.4 us
  Pallas kernels  84.1 us (93%)
  other arithmetic  3.41 us (4%)
  local copies, waits for them, and re-layouts  1.52 us (2%)
  between operations  1.41 us (2%)
    pallas_call x1, Pallas kernels, body(): pl.pallas_call(functools.partial(kernel, parts, groups, coef), out_shape=...  84.1 us
    add x1, other arithmetic, body(): teacher_next = momentum * teacher_proto + (1.0 - momentum) * student_next  2.82 us

profile of v5, /device:TPU:0, one launch (start us, length us, event | category | flops | bytes accessed | tf_op | source)
XLA Modules:
  0.0 90.4 jit_solution(13450039699289796254)
XLA Ops:
  1.4 0.0 copy-start.3
  1.4 0.6 pad_maximum_fusion.plan_ref
  2.0 0.1 copy-done.3
  2.1 0.8 copy.9.crops_ref
  2.8 0.0 copy-start
  2.8 0.0 copy-start.1
  2.8 84.1 %shard_map.85 = (f32[32,8192]{1,0:T(8,128)}, f32[160,256]{1,0:T(8,128)}) custom-call(f32[2]{0:T(128)} %pad_maximum_fusion.plan_ref, f32[160,256]{1,0:T(8,128)} %sf_ref.1, f32[32,256]{1,0:T(8,128)} %tf_ref.1, f32[32,8192]{1,0:T(8,128)} %sp_ref.1, f32[32,8192]{1,0:T(8,128)} %tp_ref.1, s32[160,2]{1,0:T(8,128)} %copy.9.crops_ref, s32[2,160]{1,0:T(2,128)} %bitcast.3), custom_call_target="tpu_custom_call" | custom-call | tf_op jit(solution)/shard_map/pallas_call | solution.py:377
  86.9 0.0 copy-done
  86.9 0.0 copy-done.1
  86.9 0.0 copy-start.2
  86.9 2.8 %multiply_add_fusion = (f32[32,8192]{1,0:T(8,128)}, f32[32,8192]{1,0:T(8,128)}) fusion(f32[32,8192]{1,0:T(8,128)S(1)} %copy-done, f32[]{:T(128)S(6)} %sub.11, f32[]{:T(128)} %bitcast.2, f32[32,8192]{1,0:T(8,128)S(1)} %copy-done.1, f32[32,8192]{1,0:T(8,128)} %get-tuple-element.5, f32[]{:T(128)} %bitcast), kind=kLoop, calls=%fused_computation | loop fusion | flops 1835008 | bytes 5242892 | tf_op jit(solution)/shard_map/add | solution.py:405
  89.7 0.0 copy-done.2
  89.7 0.7 copy.12
Async XLA Ops:
  1.4 0.7 copy-start.3
  2.8 84.1 %copy-start = (f32[32,8192]{1,0:T(8,128)S(1)}, f32[32,8192]{1,0:T(8,128)}, u32[]{:S(2)}) copy-start(f32[32,8192]{1,0:T(8,128)} %tp_ref.1) | copy-start | bytes 3145732
  2.8 84.1 %copy-start.1 = (f32[32,8192]{1,0:T(8,128)S(1)}, f32[32,8192]{1,0:T(8,128)}, u32[]{:S(2)}) copy-start(f32[32,8192]{1,0:T(8,128)} %sp_ref.1) | copy-start | bytes 3145732
  86.9 2.8 %copy-start.2 = (f32[160,256]{1,0:T(8,128)S(1)}, f32[160,256]{1,0:T(8,128)}, u32[]{:S(2)}) copy-start(f32[160,256]{1,0:T(8,128)} %get-tuple-element.14) | copy-start | bytes 491524

commit v6 on v5

--- a/solution.py
+++ b/solution.py
@@ -60,8 +60,7 @@
 
 
 def fold(values):
-    rows, columns = values.shape
-    return jnp.sum(values.reshape(rows // SUBLANES, SUBLANES, columns), axis=0)
+    return jnp.sum(values, axis=0, keepdims=True)
 
 
 def kernel(
@@ -70,7 +69,7 @@
     step_ref, fgrad_ref,
     sp_in, tp_in, s_in, t_in, own_s, own_t, unit_hi, unit_lo, expo_hi, expo_lo,
     s_hi, s_lo, lane_part, counted, counted_t, mixed_t, assign, row_dp, row_pr, tot_dp, tot_pr,
-    f_send, f_pair, f_dp, f_part, f_pr, f_sum, g_send, g_dp, g_pr, moved,
+    inv_norm, f_send, f_pair, f_dp, f_part, f_pr, f_sum, g_send, g_dp, g_pr, moved,
     dp_send, dp_recv, pr_send, pr_recv, local_sem,
 ):
     me, mine = lax.axis_index("dp"), lax.axis_index("proto")
@@ -171,7 +170,7 @@
 
     def result(moves, second):
         arrive(moves)
-        return jnp.sum(jnp.sum(second[...], axis=0), axis=0, keepdims=True)
+        return jnp.sum(second[...], axis=0)
 
     def balance(scale):
         values = assign[...]
@@ -216,8 +215,8 @@
 
     arrive(teacher_moves)
     teacher_cols = tp_in[...]
-    teacher_norm = jnp.sqrt(jnp.sum(teacher_cols * teacher_cols, axis=0, keepdims=True) + norm_eps)
-    assign[...] = jnp.exp(dot((teacher_cols / teacher_norm).T, t_in[...], NT) / temp)
+    inverse = 1.0 / jnp.sqrt(jnp.sum(teacher_cols * teacher_cols, axis=0, keepdims=True) + norm_eps)
+    assign[...] = jnp.exp(dot((teacher_cols * inverse).T, t_in[...], NT) * (1.0 / temp))
     near = first_hop(balance(None), row_dp.at[0], 4)
     near_move = start([dp_move(3, 0, partner, own_s, s_in.at[me])])
     twin_moves = start([dp_move(3, hop + 1, peer, own_s, s_in.at[me]) for hop, peer in enumerate(twins)])
@@ -250,8 +249,9 @@
 
     arrive(proto_moves)
     student_cols = sp_in[...]
-    student_norm = jnp.sqrt(jnp.sum(student_cols * student_cols, axis=0, keepdims=True) + norm_eps)
-    high, low = split(student_cols / student_norm)
+    inverse = 1.0 / jnp.sqrt(jnp.sum(student_cols * student_cols, axis=0, keepdims=True) + norm_eps)
+    inv_norm[...] = jnp.broadcast_to(inverse, inv_norm.shape)
+    high, low = split(student_cols * inverse)
     unit_hi[...] = high
     unit_lo[...] = low
     lax.fori_loop(0, half, score_tile, 0)
@@ -264,6 +264,11 @@
     scale = 1.0 / result(near, row_pr.at[2])
     mixed_pieces = split(mixed_t[...] * scale)
     g_send[...] = (targets * scale).T
+    g_moves = start([
+        dp_move(11, hop, peer, g_send.at[rows(peer, teach_rows), :], g_dp.at[me])
+        for hop, peer in enumerate(dp_peers)
+    ])
+    g_dp[me] = g_send[rows(me, teach_rows), :]
     f_near = [f_move(step) for step in range(half // 2)]
     arrive(f_near)
     sends.extend(f_near)
@@ -289,11 +294,11 @@
             - dot3(mixed_pieces, split(assign[at, :]), NT)
         )
         now = sp_in[:, at]
-        norm = jnp.sqrt(jnp.sum(now * now, axis=0, keepdims=True) + norm_eps)
-        unit = now / norm
-        proto_grad = (grad - unit * jnp.sum(unit * grad, axis=0, keepdims=True)) / norm
+        inverse = inv_norm[0:1, at]
+        unit = now * inverse
+        proto_grad = (grad - unit * jnp.sum(unit * grad, axis=0, keepdims=True)) * inverse
         square = jnp.sum(proto_grad * proto_grad, axis=0, keepdims=True) / width
-        moved[:, at] = proto_grad / jnp.sqrt(square + square_eps)
+        moved[:, at] = proto_grad * (1.0 / jnp.sqrt(square + square_eps))
         place = pl.ds(pl.multiple_of(me * share + piece * chunk, chunk), chunk)
         back_moves += start([
             dp_move(12 + piece, hop, peer, moved.at[rows(peer, own_rows), at], step_ref.at[:, place])
@@ -301,12 +306,6 @@
         ])
         home_moves.append(pltpu.make_async_copy(moved.at[own_block, at], step_ref.at[:, place], local_sem.at[2 + piece]))
         home_moves[-1].start()
-        if piece == 0:
-            g_moves = start([
-                dp_move(11, hop, peer, g_send.at[rows(peer, teach_rows), :], g_dp.at[me])
-                for hop, peer in enumerate(dp_peers)
-            ])
-            g_dp[me] = g_send[rows(me, teach_rows), :]
         if piece == 1:
             arrive(f_moves)
             f_part[0:crop_rows, :] = jnp.sum(f_dp[...], axis=0)
@@ -388,9 +387,9 @@
             vmem(all_s, width, dtype=bf16), vmem(all_s, width, dtype=bf16),
             vmem(all_s, LANES), vmem(all_s, width), vmem(width, all_s), vmem(width, all_t),
             vmem(share, all_t),
-            vmem(ITERS, parts, SUBLANES, all_t), vmem(ITERS, groups, SUBLANES, all_t),
-            vmem(parts, SUBLANES, all_s), vmem(groups, SUBLANES, all_s),
-            vmem(all_s, width), vmem(all_s // 2, width),
+            vmem(ITERS, parts, 1, all_t), vmem(ITERS, groups, 1, all_t),
+            vmem(parts, 1, all_s), vmem(groups, 1, all_s),
+            vmem(SUBLANES, share), vmem(all_s, width), vmem(all_s // 2, width),
             vmem(parts // 2, crop_rows, width), vmem(groups * piece_rows, width),
             vmem(groups, piece_rows, width), vmem(groups * piece_rows, width),
             vmem(all_t, width), vmem(parts, teach_rows, width), vmem(groups, teach_rows, width),

time: 90.6 us -> 89.5 us (0.988)
  Pallas kernels: 84.1 us -> 83 us
    pallas_call x1, Pallas kernels: 84.1 us -> 83 us  [body(): pl.pallas_call(functools.partial(kernel, parts, groups, coef), out_shape=...]
where the time goes in v6:
time: 89.5 us; the launch traced here: 89.3 us
  Pallas kernels  83 us (93%)
  other arithmetic  3.41 us (4%)
  local copies, waits for them, and re-layouts  1.52 us (2%)
  between operations  1.41 us (2%)
    pallas_call x1, Pallas kernels, body(): pl.pallas_call(functools.partial(kernel, parts, groups, coef), out_shape=...  83 us
    add x1, other arithmetic, body(): teacher_next = momentum * teacher_proto + (1.0 - momentum) * student_next  2.82 us

profile of v6, /device:TPU:0, one launch (start us, length us, event | category | flops | bytes accessed | tf_op | source)
XLA Modules:
  0.0 89.3 jit_solution(5612034873875029653)
XLA Ops:
  1.4 0.0 copy-start.3
  1.4 0.6 pad_maximum_fusion.plan_ref
  2.0 0.1 copy-done.3
  2.1 0.8 copy.9.crops_ref
  2.8 0.0 copy-start
  2.8 0.0 copy-start.1
  2.8 83.0 %shard_map.85 = (f32[32,8192]{1,0:T(8,128)}, f32[160,256]{1,0:T(8,128)}) custom-call(f32[2]{0:T(128)} %pad_maximum_fusion.plan_ref, f32[160,256]{1,0:T(8,128)} %sf_ref.1, f32[32,256]{1,0:T(8,128)} %tf_ref.1, f32[32,8192]{1,0:T(8,128)} %sp_ref.1, f32[32,8192]{1,0:T(8,128)} %tp_ref.1, s32[160,2]{1,0:T(8,128)} %copy.9.crops_ref, s32[2,160]{1,0:T(2,128)} %bitcast.3), custom_call_target="tpu_custom_call" | custom-call | tf_op jit(solution)/shard_map/pallas_call | solution.py:376
  85.8 0.0 copy-done
  85.8 0.0 copy-done.1
  85.8 0.0 copy-start.2
  85.9 2.8 %multiply_add_fusion = (f32[32,8192]{1,0:T(8,128)}, f32[32,8192]{1,0:T(8,128)}) fusion(f32[32,8192]{1,0:T(8,128)S(1)} %copy-done, f32[]{:T(128)S(6)} %sub.11, f32[]{:T(128)} %bitcast.2, f32[32,8192]{1,0:T(8,128)S(1)} %copy-done.1, f32[32,8192]{1,0:T(8,128)} %get-tuple-element.5, f32[]{:T(128)} %bitcast), kind=kLoop, calls=%fused_computation | loop fusion | flops 1835008 | bytes 5242892 | tf_op jit(solution)/shard_map/add | solution.py:404
  88.7 0.0 copy-done.2
  88.7 0.7 copy.12
Async XLA Ops:
  1.4 0.7 copy-start.3
  2.8 83.0 %copy-start = (f32[32,8192]{1,0:T(8,128)S(1)}, f32[32,8192]{1,0:T(8,128)}, u32[]{:S(2)}) copy-start(f32[32,8192]{1,0:T(8,128)} %tp_ref.1) | copy-start | bytes 3145732
  2.8 83.0 %copy-start.1 = (f32[32,8192]{1,0:T(8,128)S(1)}, f32[32,8192]{1,0:T(8,128)}, u32[]{:S(2)}) copy-start(f32[32,8192]{1,0:T(8,128)} %sp_ref.1) | copy-start | bytes 3145732
  85.8 2.8 %copy-start.2 = (f32[160,256]{1,0:T(8,128)S(1)}, f32[160,256]{1,0:T(8,128)}, u32[]{:S(2)}) copy-start(f32[160,256]{1,0:T(8,128)} %get-tuple-element.14) | copy-start | bytes 491524

commit v7 on v6

--- a/solution.py
+++ b/solution.py
@@ -65,11 +65,11 @@
 
 def kernel(
     parts, groups, coef,
-    plan_ref, sf_ref, tf_ref, sp_ref, tp_ref, crops_ref, crops_t_ref,
+    plan_ref, sf_ref, tf_ref, sp_ref, tp_ref, crops_ref,
     step_ref, fgrad_ref,
     sp_in, tp_in, s_in, t_in, own_s, own_t, unit_hi, unit_lo, expo_hi, expo_lo,
     s_hi, s_lo, lane_part, counted, counted_t, mixed_t, assign, row_dp, row_pr, tot_dp, tot_pr,
-    inv_norm, f_send, f_pair, f_dp, f_part, f_pr, f_sum, g_send, g_dp, g_pr, moved,
+    pair_pad, inv_norm, f_send, f_pair, f_dp, f_part, f_pr, f_sum, g_send, g_dp, g_pr, moved,
     dp_send, dp_recv, pr_send, pr_recv, local_sem,
 ):
     me, mine = lax.axis_index("dp"), lax.axis_index("proto")
@@ -78,7 +78,7 @@
     own_rows, columns = sp_ref.shape
     share = columns // parts
     half = parts // 2
-    temp = plan_ref[1]
+    temp = 0.04 + 0.03 * jnp.minimum(1.0, plan_ref[0].astype(f32) / WARM_STEPS)
     parity = lax.rem(me, 2)
     partner = me + 1 - 2 * parity
     twins = [lax.rem(me + 2 * hop, parts) for hop in range(1, half)]
@@ -140,10 +140,12 @@
     s_values = sf_ref[...]
     s_norm = jnp.sqrt(jnp.sum(s_values * s_values, axis=1, keepdims=True) + norm_eps)
     s_unit = s_values / s_norm
-    teach = lax.broadcasted_iota(jnp.int32, (teach_rows, crop_rows), 0)
-    same = crops_t_ref[0:1, :] == teach // GLOBAL_CROPS
-    other = crops_t_ref[1:2, :] != teach % GLOBAL_CROPS
-    pairs_t = jnp.where(same & other, 1.0, 0.0).astype(f32)
+    teach = lax.broadcasted_iota(jnp.int32, (crop_rows, pair_pad.shape[1]), 1)
+    same = crops_ref[:, 0:1] == teach // GLOBAL_CROPS
+    other = crops_ref[:, 1:2] != teach % GLOBAL_CROPS
+    pair_pad[...] = jnp.zeros(pair_pad.shape, f32)
+    pair_pad[0:crop_rows, :] = jnp.where(same & other & (teach < teach_rows), 1.0, 0.0).astype(f32)
+    pairs_t = pair_pad[...].T[0:teach_rows, 0:crop_rows]
     mixed_at, count_at = crop_rows, crop_rows + teach_rows
     own_s[0:crop_rows, :] = s_unit
     own_s[mixed_at:count_at, :] = dot(pairs_t, s_unit, NN)
@@ -186,18 +188,30 @@
     def place_of(block):
         return (block // 2) + half * lax.rem(block, 2)
 
-    def score_tile(step, carry):
-        at = rows(step, tile)
-        unit = (unit_hi[...], unit_lo[...])
-        expo = jnp.exp(dot3((s_hi[at, :], s_lo[at, :]), unit, NN) / student_temp)
-        part = expo[:, 0:LANES]
-        for lane in range(1, share // LANES):
-            part = part + expo[:, lane * LANES:(lane + 1) * LANES]
-        lane_part[at, :] = part
-        pieces = split(expo)
-        expo_hi[at, :] = pieces[0]
-        expo_lo[at, :] = pieces[1]
-        return carry
+    def scores(side):
+        at_cols = slice(side * wide, (side + 1) * wide)
+        arrive(proto_moves[side])
+        now = sp_in[:, at_cols]
+        inverse = 1.0 / jnp.sqrt(jnp.sum(now * now, axis=0, keepdims=True) + norm_eps)
+        inv_norm[:, at_cols] = jnp.broadcast_to(inverse, (SUBLANES, wide))
+        high, low = split(now * inverse)
+        unit_hi[:, at_cols] = high
+        unit_lo[:, at_cols] = low
+
+        def score_tile(step, carry):
+            at = rows(step, tile)
+            unit = (unit_hi[:, at_cols], unit_lo[:, at_cols])
+            expo = jnp.exp(dot3((s_hi[at, :], s_lo[at, :]), unit, NN) * (1.0 / student_temp))
+            part = expo[:, 0:LANES]
+            for lane in range(1, wide // LANES):
+                part = part + expo[:, lane * LANES:(lane + 1) * LANES]
+            lane_part[at, :] = part if side == 0 else lane_part[at, :] + part
+            pieces = split(expo)
+            expo_hi[at, at_cols] = pieces[0]
+            expo_lo[at, at_cols] = pieces[1]
+            return carry
+
+        lax.fori_loop(0, half, score_tile, 0)
 
     def f_move(step):
         at = pl.ds(pl.multiple_of((1 - parity) * half_rows + step * tile, tile), tile)
@@ -223,9 +237,17 @@
     near = second_hop(near, row_dp.at[0], row_pr.at[0], 0)
     scale = 1.0 / result(near, row_pr.at[0])
     near = first_hop(balance(scale), row_dp.at[1], 5)
-    proto_moves = start(
-        [dp_move(2, hop, peer, sp_ref.at[:, cols(peer)], sp_in.at[own_block, :]) for hop, peer in enumerate(dp_peers)]
-    )
+    wide = share // 2
+    proto_moves = []
+    for side in range(2):
+        proto_moves.append(start([
+            dp_move(
+                (2, 12 + CHUNKS)[side], hop, peer,
+                sp_ref.at[:, pl.ds(pl.multiple_of(peer * share + side * wide, wide), wide)],
+                sp_in.at[own_block, side * wide:(side + 1) * wide],
+            )
+            for hop, peer in enumerate(dp_peers)
+        ]))
     arrive(twin_moves)
     onward = start(
         [dp_move(8, hop, partner, s_in.at[block], s_in.at[block]) for hop, block in enumerate(senders)]
@@ -243,18 +265,11 @@
         counted[at, :] = crops_now * jnp.concatenate([count[0:crop_rows, :]] * (width // LANES), axis=1)
     counted_t[...] = counted[...].T
     mixed_t[...] = s_in[:, mixed_at:count_at, :].reshape(parts * teach_rows, width).T
-
+    scores(0)
     scale = 1.0 / result(near, row_pr.at[1])
     near = first_hop(balance(scale), row_dp.at[2], 6)
 
-    arrive(proto_moves)
-    student_cols = sp_in[...]
-    inverse = 1.0 / jnp.sqrt(jnp.sum(student_cols * student_cols, axis=0, keepdims=True) + norm_eps)
-    inv_norm[...] = jnp.broadcast_to(inverse, inv_norm.shape)
-    high, low = split(student_cols * inverse)
-    unit_hi[...] = high
-    unit_lo[...] = low
-    lax.fori_loop(0, half, score_tile, 0)
+    scores(1)
     tot_near = first_hop(fold(lane_part[...].T), tot_dp, 7)
     near = second_hop(near, row_dp.at[2], row_pr.at[2], 2)
     feature_tiles(1 - parity, True)
@@ -361,7 +376,7 @@
     coef = loss_scale / (pair_total * images * student_temp)
     all_s, all_t = parts * crop_rows, parts * teach_rows
     packed = crop_rows + teach_rows + SUBLANES
-    kinds = 12 + CHUNKS
+    kinds = 13 + CHUNKS
     piece_rows = -(-crop_rows // (groups * SUBLANES)) * SUBLANES
     rate, teacher_temp, momentum = plan(step)
 
@@ -376,7 +391,7 @@
     direction, feature_grad = pl.pallas_call(
         functools.partial(kernel, parts, groups, coef),
         out_shape=[jax.ShapeDtypeStruct(one.shape, f32) for one in shapes],
-        in_specs=[pl.BlockSpec(memory_space=pltpu.SMEM), whole, whole, outside, outside, whole, whole],
+        in_specs=[pl.BlockSpec(memory_space=pltpu.SMEM), whole, whole, outside, outside, whole],
         out_specs=[outside, whole],
         scratch_shapes=[
             vmem(width, share), vmem(width, share),
@@ -389,6 +404,7 @@
             vmem(share, all_t),
             vmem(ITERS, parts, 1, all_t), vmem(ITERS, groups, 1, all_t),
             vmem(parts, 1, all_s), vmem(groups, 1, all_s),
+            vmem(-(-crop_rows // LANES) * LANES, -(-teach_rows // LANES) * LANES),
             vmem(SUBLANES, share), vmem(all_s, width), vmem(all_s // 2, width),
             vmem(parts // 2, crop_rows, width), vmem(groups * piece_rows, width),
             vmem(groups, piece_rows, width), vmem(groups * piece_rows, width),
@@ -399,7 +415,7 @@
         compiler_params=pltpu.CompilerParams(
             collective_id=0, has_side_effects=True, vmem_limit_bytes=56 * 1024 * 1024
         ),
-    )(jnp.stack([rate, teacher_temp]), student_feats, teacher_feats, student_proto, teacher_proto, crops, crops.T)
+    )(step, student_feats, teacher_feats, student_proto, teacher_proto, crops)
     student_next = student_proto - rate * (direction + weight_decay * student_proto)
     teacher_next = momentum * teacher_proto + (1.0 - momentum) * student_next
     return (student_next, teacher_next, feature_grad)

time: 89.5 us -> 88.2 us (0.985)
  Pallas kernels: 83 us -> 81.7 us
    pallas_call x1, Pallas kernels: 83 us -> 81.7 us  [body(): pl.pallas_call(functools.partial(kernel, parts, groups, coef), out_shape=...]
where the time goes in v7:
time: 88.2 us; the launch traced here: 88 us
  Pallas kernels  81.7 us (93%)
  other arithmetic  2.82 us (3%)
  local copies, waits for them, and re-layouts  2.11 us (2%)
  between operations  1.41 us (2%)
    pallas_call x1, Pallas kernels, body(): pl.pallas_call(functools.partial(kernel, parts, groups, coef), out_shape=...  81.7 us
    add x1, other arithmetic, body(): teacher_next = momentum * teacher_proto + (1.0 - momentum) * student_next  2.82 us
    unnamed x10, local copies, waits for them, and re-layouts  2.11 us

profile of v7, /device:TPU:0, one launch (start us, length us, event | category | flops | bytes accessed | tf_op | source)
XLA Modules:
  0.0 88.0 jit_solution(17302725318545618371)
XLA Ops:
  1.4 0.0 copy-start.3
  1.4 0.7 copy-done.3
  2.0 0.8 copy.9.crops_ref
  2.8 0.0 copy-start
  2.8 0.0 copy-start.1
  2.8 81.7 %shard_map.85 = (f32[32,8192]{1,0:T(8,128)}, f32[160,256]{1,0:T(8,128)}) custom-call(s32[1]{0:T(128)S(6)} %copy.11.plan_ref, f32[160,256]{1,0:T(8,128)} %sf_ref.1, f32[32,256]{1,0:T(8,128)} %tf_ref.1, f32[32,8192]{1,0:T(8,128)} %sp_ref.1, f32[32,8192]{1,0:T(8,128)} %tp_ref.1, s32[160,2]{1,0:T(8,128)} %copy.9.crops_ref), custom_call_target="tpu_custom_call" | custom-call | tf_op jit(solution)/shard_map/pallas_call | solution.py:391
  84.5 0.0 copy-done
  84.5 0.0 copy-done.1
  84.5 0.0 copy-start.2
  84.5 2.8 %multiply_add_fusion = (f32[32,8192]{1,0:T(8,128)}, f32[32,8192]{1,0:T(8,128)}) fusion(f32[32,8192]{1,0:T(8,128)S(1)} %copy-done, f32[]{:T(128)S(6)} %sub.11, f32[]{:T(128)} %bitcast.1, f32[32,8192]{1,0:T(8,128)S(1)} %copy-done.1, f32[32,8192]{1,0:T(8,128)} %get-tuple-element.5, f32[]{:T(128)} %bitcast), kind=kLoop, calls=%fused_computation | loop fusion | flops 1835008 | bytes 5242892 | tf_op jit(solution)/shard_map/add | solution.py:420
  87.3 0.0 copy-done.2
  87.3 0.7 copy.12
Async XLA Ops:
  1.4 0.7 copy-start.3
  2.8 81.7 %copy-start = (f32[32,8192]{1,0:T(8,128)S(1)}, f32[32,8192]{1,0:T(8,128)}, u32[]{:S(2)}) copy-start(f32[32,8192]{1,0:T(8,128)} %tp_ref.1) | copy-start | bytes 3145732
  2.8 81.7 %copy-start.1 = (f32[32,8192]{1,0:T(8,128)S(1)}, f32[32,8192]{1,0:T(8,128)}, u32[]{:S(2)}) copy-start(f32[32,8192]{1,0:T(8,128)} %sp_ref.1) | copy-start | bytes 3145732
  84.5 2.8 %copy-start.2 = (f32[160,256]{1,0:T(8,128)S(1)}, f32[160,256]{1,0:T(8,128)}, u32[]{:S(2)}) copy-start(f32[160,256]{1,0:T(8,128)} %get-tuple-element.14) | copy-start | bytes 491524

commit v8 on v7

--- a/solution.py
+++ b/solution.py
@@ -275,15 +275,6 @@
     feature_tiles(1 - parity, True)
     tot_near = second_hop(tot_near, tot_dp, tot_pr, 3)
     feature_tiles(parity, False)
-    targets = dot3((unit_hi[...], unit_lo[...]), split(assign[...]), NN)
-    scale = 1.0 / result(near, row_pr.at[2])
-    mixed_pieces = split(mixed_t[...] * scale)
-    g_send[...] = (targets * scale).T
-    g_moves = start([
-        dp_move(11, hop, peer, g_send.at[rows(peer, teach_rows), :], g_dp.at[me])
-        for hop, peer in enumerate(dp_peers)
-    ])
-    g_dp[me] = g_send[rows(me, teach_rows), :]
     f_near = [f_move(step) for step in range(half // 2)]
     arrive(f_near)
     sends.extend(f_near)
@@ -295,6 +286,15 @@
         for hop, peer in enumerate(twins)
     ])
     f_dp[slot] = f_send[rows(place_of(me), crop_rows), :]
+    targets = dot3((unit_hi[...], unit_lo[...]), split(assign[...]), NN)
+    scale = 1.0 / result(near, row_pr.at[2])
+    mixed_pieces = split(mixed_t[...] * scale)
+    g_send[...] = (targets * scale).T
+    g_moves = start([
+        dp_move(11, hop, peer, g_send.at[rows(peer, teach_rows), :], g_dp.at[me])
+        for hop, peer in enumerate(dp_peers)
+    ])
+    g_dp[me] = g_send[rows(me, teach_rows), :]
     inverse_row = 1.0 / result(tot_near, tot_pr)
     weighted_t = split(counted_t[...] * inverse_row)
     lane_part[...] = jnp.broadcast_to(inverse_row, (LANES, parts * crop_rows)).T

time: 88.2 us -> 86.1 us (0.976)
  Pallas kernels: 81.7 us -> 79.6 us
    pallas_call x1, Pallas kernels: 81.7 us -> 79.6 us  [body(): pl.pallas_call(functools.partial(kernel, parts, groups, coef), out_shape=...]
where the time goes in v8:
time: 86.1 us; the launch traced here: 85.9 us
  Pallas kernels  79.6 us (92%)
  other arithmetic  2.82 us (3%)
  local copies, waits for them, and re-layouts  2.11 us (2%)
  between operations  1.41 us (2%)
    pallas_call x1, Pallas kernels, body(): pl.pallas_call(functools.partial(kernel, parts, groups, coef), out_shape=...  79.6 us
    add x1, other arithmetic, body(): teacher_next = momentum * teacher_proto + (1.0 - momentum) * student_next  2.82 us
    unnamed x10, local copies, waits for them, and re-layouts  2.11 us

profile of v8, /device:TPU:0, one launch (start us, length us, event | category | flops | bytes accessed | tf_op | source)
XLA Modules:
  0.0 85.9 jit_solution(2005727252439506669)
XLA Ops:
  1.4 0.0 copy-start.3
  1.4 0.7 copy-done.3
  2.0 0.8 copy.9.crops_ref
  2.8 0.0 copy-start
  2.8 0.0 copy-start.1
  2.8 79.6 %shard_map.85 = (f32[32,8192]{1,0:T(8,128)}, f32[160,256]{1,0:T(8,128)}) custom-call(s32[1]{0:T(128)S(6)} %copy.11.plan_ref, f32[160,256]{1,0:T(8,128)} %sf_ref.1, f32[32,256]{1,0:T(8,128)} %tf_ref.1, f32[32,8192]{1,0:T(8,128)} %sp_ref.1, f32[32,8192]{1,0:T(8,128)} %tp_ref.1, s32[160,2]{1,0:T(8,128)} %copy.9.crops_ref), custom_call_target="tpu_custom_call" | custom-call | tf_op jit(solution)/shard_map/pallas_call | solution.py:391
  82.4 0.0 copy-done
  82.4 0.0 copy-done.1
  82.4 0.0 copy-start.2
  82.4 2.8 %multiply_add_fusion = (f32[32,8192]{1,0:T(8,128)}, f32[32,8192]{1,0:T(8,128)}) fusion(f32[32,8192]{1,0:T(8,128)S(1)} %copy-done, f32[]{:T(128)S(6)} %sub.11, f32[]{:T(128)} %bitcast.1, f32[32,8192]{1,0:T(8,128)S(1)} %copy-done.1, f32[32,8192]{1,0:T(8,128)} %get-tuple-element.5, f32[]{:T(128)} %bitcast), kind=kLoop, calls=%fused_computation | loop fusion | flops 1835008 | bytes 5242892 | tf_op jit(solution)/shard_map/add | solution.py:420
  85.2 0.0 copy-done.2
  85.2 0.7 copy.12
Async XLA Ops:
  1.4 0.7 copy-start.3
  2.8 79.6 %copy-start = (f32[32,8192]{1,0:T(8,128)S(1)}, f32[32,8192]{1,0:T(8,128)}, u32[]{:S(2)}) copy-start(f32[32,8192]{1,0:T(8,128)} %tp_ref.1) | copy-start | bytes 3145732
  2.8 79.6 %copy-start.1 = (f32[32,8192]{1,0:T(8,128)S(1)}, f32[32,8192]{1,0:T(8,128)}, u32[]{:S(2)}) copy-start(f32[32,8192]{1,0:T(8,128)} %sp_ref.1) | copy-start | bytes 3145732
  82.4 2.8 %copy-start.2 = (f32[160,256]{1,0:T(8,128)S(1)}, f32[160,256]{1,0:T(8,128)}, u32[]{:S(2)}) copy-start(f32[160,256]{1,0:T(8,128)} %get-tuple-element.14) | copy-start | bytes 491524
